TPU v7x, 32 devices: a whole 2x2x4 slice. The times are simulated.
32 devices in a mesh: rep: 16 (over z, y, x), tp: 2 (over core).
Axes of the slice: x: 2, y: 2, z: 4, core: 2. Of those that a mesh axis runs over, the one named last changes fastest.
Arguments:
- lookup_vectors: bfloat16 [4, 64, 128, 128], P(None, 'rep', 'tp'), may hold values from -5 to 5
- fresh_token_memory: bfloat16 [4, 64, 2, 8, 128], P(None, 'rep', None, 'tp'), may hold values from -5 to 5
- unfinished_block_memory: bfloat16 [64, 2, 16, 8, 128], P('rep', None, None, 'tp'), may hold values from -5 to 5
- cache_block_store: bfloat16 [1024, 2, 16, 8, 128], P('rep', None, None, 'tp'), may hold values from -7.5 to 7.5
- sequence_block_index: int32 [64, 128], P('rep'), may hold values from 0 to 191
- sequence_history_count: int32 [64], P('rep'), may hold values from 1 to 2048, as said below
- unfinished_block_fill: int32 [64], P('rep'), may hold values from 0 to 12
- migration_sender_block: int32 [1024], P('rep'), may hold values from 0 to 67
- migration_receiver_server: int32 [1024, 1], P('rep'), may hold values from 0 to 15; in each aligned block of 64 rows (0 to 63, 64 to 127, ...) at most 8 rows name the same one
- switch_moment: int32 [64], P('rep'), may hold values from 0 to 4
- output_scaling_weights: float32 [16384], P('tp'), may hold values from 0.5 to 1.5
Outputs:
- normed: bfloat16 [4, 64, 16384], P(None, 'rep', 'tp')
Inputs may be any that keep to these rules, and one draw needn't show every extreme that they name: `sequence_block_index`: an entry below 64 names a page of the request's own replica, an entry 64 + j its arrival slot j. `sequence_history_count`: some request holds the full 128 * 16 tokens in every draw. `migration_sender_block`: an entry below 64 names a page of the replica's own pool, an entry 64 + i the tail page of its request i. `migration_receiver_server`: among the 64 entries of one replica no destination appears more than 8 times.
All inputs are finite; a program needn't handle non-finite values.
Results may differ from a plain program's by a relative error of at most 0.0056.
Values may be sent and summed in bfloat16 or wider, within the bound.
A program may use at most 64 MiB of HBM per device.

v0:
```python
import math

import jax
import jax.numpy as jnp
from jax import lax
from jax.sharding import PartitionSpec as P


def filled_tail(unfinished_block_memory, fresh_token_memory, unfinished_block_fill):
    decode_steps = fresh_token_memory.shape[0]
    page_entry = unfinished_block_memory.shape[2]
    offsets = jnp.arange(page_entry, dtype=jnp.int32)
    hits = (
        offsets[None, None, :]
        == unfinished_block_fill[None, :, None]
        + jnp.arange(decode_steps, dtype=jnp.int32)[:, None, None]
    )
    placed = jnp.einsum(
        "srp,srckd->rcpkd",
        hits.astype(jnp.bfloat16),
        fresh_token_memory,
        preferred_element_type=jnp.float32,
    )
    covered = jnp.any(hits, axis=0)
    return jnp.where(
        covered[:, None, :, None, None], placed.astype(jnp.bfloat16), unfinished_block_memory
    )


def slot_ranks(target):
    order = jnp.arange(target.shape[0], dtype=jnp.int32)
    same = (target[:, None] == target[None, :]) & (order[None, :] < order[:, None])
    return jnp.sum(same.astype(jnp.int32), axis=1, dtype=jnp.int32)


def pick_rows(selector, table):
    flat = table.reshape(table.shape[0], -1)
    picked = jnp.dot(selector.astype(jnp.bfloat16), flat, preferred_element_type=jnp.float32)
    return picked.astype(jnp.bfloat16).reshape((selector.shape[0],) + table.shape[1:])


def one_hot_rows(index, count):
    return index[:, None] == jnp.arange(count, dtype=jnp.int32)[None, :]


def token_validity(
    page_table_row,
    context_length,
    arrival_length,
    tail_length,
    boundary_marker,
    pool_page_tiles,
    page_entry,
    decode_steps,
):
    entry = jnp.repeat(page_table_row, page_entry)
    position = jnp.arange(entry.shape[0], dtype=jnp.int32)
    offset = position % page_entry
    incoming = entry >= pool_page_tiles
    known = arrival_length[jnp.clip(entry - pool_page_tiles, 0, arrival_length.shape[0] - 1)]
    step = jnp.arange(decode_steps, dtype=jnp.int32)[:, None]
    page_ok = (position < context_length)[None, :] & (
        jnp.logical_not(incoming)[None, :] | (step >= boundary_marker) & (offset < known)[None, :]
    )
    tail_ok = jnp.arange(page_entry, dtype=jnp.int32)[None, :] < tail_length + step + 1
    return jnp.concatenate([page_ok, tail_ok], axis=1)


def attend(query_vector, pages, tail_block, valid_mask):
    decode_steps, heads, hdim = query_vector.shape
    kv_heads = pages.shape[3]
    keys = jnp.concatenate([pages[:, 0].reshape(-1, kv_heads, hdim), tail_block[0]], 0)
    values = jnp.concatenate([pages[:, 1].reshape(-1, kv_heads, hdim), tail_block[1]], 0)
    grouped = query_vector.reshape(decode_steps, kv_heads, heads // kv_heads, hdim)
    scores = jnp.einsum(
        "skgd,lkd->skgl", grouped, keys, preferred_element_type=jnp.float32
    ) / math.sqrt(hdim)
    scores = jnp.where(valid_mask[:, None, None, :], scores, -jnp.inf)
    top = jnp.max(scores, axis=-1, keepdims=True)
    probs = jnp.exp(scores - top)
    total = jnp.sum(probs, axis=-1, keepdims=True)
    weights = probs.astype(jnp.bfloat16)
    mixed = (
        jnp.einsum("skgl,lkd->skgd", weights, values, preferred_element_type=jnp.float32) / total
    )
    return mixed.reshape(decode_steps, heads, hdim).astype(jnp.bfloat16)


def body(
    lookup_vectors,
    fresh_token_memory,
    unfinished_block_memory,
    cache_block_store,
    sequence_block_index,
    sequence_history_count,
    unfinished_block_fill,
    migration_sender_block,
    migration_receiver_server,
    switch_moment,
    output_scaling_weights,
):
    replicas = lax.axis_size("rep")
    decode_steps, requests, heads, hdim = lookup_vectors.shape
    pool_page_tiles = cache_block_store.shape[0]
    page_entry = cache_block_store.shape[2]
    entries = migration_sender_block.shape[0]
    capacity = max(2, 2 * entries // replicas)
    slot_count = replicas * capacity
    from_tail = migration_sender_block >= pool_page_tiles
    pool_pick = jnp.clip(migration_sender_block, 0, pool_page_tiles - 1)
    tail_pick = jnp.clip(migration_sender_block - pool_page_tiles, 0, requests - 1)
    lengths = jnp.where(
        from_tail, unfinished_block_fill[tail_pick] + switch_moment[tail_pick], page_entry
    )
    target = migration_receiver_server[:, 0]
    landing = target * capacity + slot_ranks(target)
    out_len = jnp.zeros((slot_count,), jnp.int32).at[landing].set(lengths)
    placement = jnp.transpose(one_hot_rows(landing, slot_count))
    pool_select = one_hot_rows(pool_pick, pool_page_tiles)
    tail_select = one_hot_rows(tail_pick, requests)
    tails = filled_tail(unfinished_block_memory, fresh_token_memory, unfinished_block_fill)
    moved = jnp.where(
        from_tail[:, None, None, None, None],
        pick_rows(tail_select, tails),
        pick_rows(pool_select, cache_block_store),
    )
    outgoing = pick_rows(placement, moved)
    arrived, arrival_length = (
        lax.all_to_all(outgoing, "rep", split_axis=0, concat_axis=0, tiled=True),
        lax.all_to_all(out_len, "rep", split_axis=0, concat_axis=0, tiled=True),
    )
    extended = jnp.concatenate([cache_block_store, arrived], 0)
    extended_count = extended.shape[0]

    def one_request(request_element):
        query_vector, page_table_row, tail_block, context_length, tail_length, handover_step = (
            request_element
        )
        valid_mask = token_validity(
            page_table_row,
            context_length,
            arrival_length,
            tail_length,
            handover_step,
            pool_page_tiles,
            page_entry,
            decode_steps,
        )
        pages = pick_rows(one_hot_rows(page_table_row, extended_count), extended)
        return attend(query_vector, pages, tail_block, valid_mask)

    mixed = lax.map(
        one_request,
        (
            jnp.transpose(lookup_vectors, (1, 0, 2, 3)),
            sequence_block_index,
            tails,
            sequence_history_count,
            unfinished_block_fill,
            switch_moment,
        ),
    )
    attn = jnp.transpose(mixed.reshape(requests, decode_steps, heads * hdim), (1, 0, 2))
    wide = attn.astype(jnp.float32)
    width = heads * hdim * lax.axis_size("tp")
    squared = lax.psum(jnp.sum(wide * wide, axis=-1, keepdims=True), "tp")
    mean = squared / width
    return (wide * lax.rsqrt(mean + 1e-05) * output_scaling_weights).astype(jnp.bfloat16)


def solution(mesh):
    placed = (
        P(None, "rep", "tp", None),
        P(None, "rep", None, "tp", None),
        P("rep", None, None, "tp", None),
        P("rep", None, None, "tp", None),
        P("rep", None),
        P("rep"),
        P("rep"),
        P("rep"),
        P("rep", None),
        P("rep"),
        P("tp"),
    )
    return jax.shard_map(
        body, mesh=mesh, in_specs=placed, out_specs=P(None, "rep", "tp"), check_vma=False
    )
```

profile of v0, /device:TPU:15, one launch (start us, length us, event | category | flops | bytes accessed | tf_op | source)
XLA Modules:
  0.0 325.5 jit_solution(9719430366530901283)
XLA Ops:
  4.5 5.6 %fusion.40 = (s32[64]{0:T(128)S(1)}, s32[64]{0:T(128)S(1)}, s32[64]{0:T(128)S(1)}) fusion(s32[]{:T(128)} %bitcast.28, s32[]{:T(128)} %bitcast.29, s32[]{:T(128)} %bitcast.30, s32[]{:T(128)} %bitcast.31, s32[]{:T(128)} %bitcast.24, s32[]{:T(128)} %bitcast.25, s32[]{:T(128)} %bitcast.26, s32[]{:T(128)} %bitcast.27, s32[64]{0:T(128)} %param.20), kind=kLoop, calls=%fused_computation.86 | loop fusion | flops 1152 | bytes 1056 | tf_op jit(solution)/shard_map/jit(_where)/select_n | solution.py:112
  11.5 6.6 %all-to-all-start.1 = ((s32[16,8,1]{1,2,0:T(1,128)}), s32[16,8,1]{1,2,0:T(1,128)S(1)}, u32[]{:S(2)}, u32[]{:S(2)}) async-start(s32[16,8,1]{1,2,0:T(1,128)} %bitcast.32), calls=%async_computation.1 | async-start | bytes 16384 | tf_op jit(solution)/shard_map/all_to_all | solution.py:130
  25.4 5.4 %convolution_convert_fusion.1 = bf16[128,16384]{1,0:T(8,128)(2,1)} fusion(bf16[64,16384]{1,0:T(8,128)(2,1)} %convolution_convert_fusion.2, bf16[4,16384]{1,0:T(4,128)(2,1)S(1)} %reshape.162, pred[64]{0:T(512)(128)(4,1)S(1)} %broadcast_compare_fusion, s32[64]{0:T(128)S(1)} %get-tuple-element.167, s32[64]{0:T(128)S(1)} %get-tuple-element.164), kind=kOutput, calls=%fused_computation.47 | convolution fusion | flops 281026816 | bytes 6423104 | tf_op jit(solution)/shard_map/dot_general | solution.py:38
  30.8 7.7 %reshape.164 = bf16[128,2,16,4,128]{4,3,2,1,0:T(4,128)(2,1)} reshape(bf16[128,16384]{1,0:T(8,128)(2,1)} %convolution_convert_fusion.1) | data formatting | bytes 8388608 | tf_op jit(solution)/shard_map/reshape | solution.py:39
  38.6 6.5 %all-to-all-start = ((bf16[128,2,16,4,128]{4,3,2,1,0:T(4,128)(2,1)}), bf16[128,2,16,4,128]{4,3,2,1,0:T(4,128)(2,1)}, u32[]{:S(2)}, u32[]{:S(2)}) async-start(bf16[128,2,16,4,128]{4,3,2,1,0:T(4,128)(2,1)} %reshape.164), calls=%async_computation | async-start | bytes 8388608 | tf_op jit(solution)/shard_map/all_to_all | solution.py:129
  46.3 92.1 %all-to-all-done = bf16[128,2,16,4,128]{4,3,2,1,0:T(4,128)(2,1)} async-done(((bf16[128,2,16,4,128]{4,3,2,1,0:T(4,128)(2,1)}), bf16[128,2,16,4,128]{4,3,2,1,0:T(4,128)(2,1)}, u32[]{:S(2)}, u32[]{:S(2)}) %all-to-all-start) | async-done | bytes 4194336 | tf_op jit(solution)/shard_map/all_to_all | solution.py:129
  138.5 8.9 %pad_maximum_fusion = bf16[192,2,16,4,128]{4,3,2,1,0:T(4,128)(2,1)} fusion(bf16[128,2,16,4,128]{4,3,2,1,0:T(4,128)(2,1)} %all-to-all-done, bf16[64,2,16,4,128]{4,3,2,1,0:T(4,128)(2,1)S(1)} %copy-done.1), kind=kLoop, calls=%fused_computation.51 | loop fusion | flops 3145728 | bytes 12582912 | tf_op jit(solution)/shard_map/concatenate | solution.py:132
  147.4 11.2 %reshape.221 = bf16[192,16384]{1,0:T(8,128)(2,1)} reshape(bf16[192,2,16,4,128]{4,3,2,1,0:T(4,128)(2,1)} %pad_maximum_fusion) | data formatting | bytes 12582912 | tf_op jit(solution)/shard_map/while/body/eval_jaxpr/reshape | solution.py:37
  158.6 161.6 %while.13 = (s32[]{:T(128)}, bf16[4,4,64,128]{3,2,1,0:T(8,128)(2,1)S(1)}, s32[4,128]{1,0:T(4,128)}, bf16[192,2,16,4,128]{4,3,2,1,0:T(4,128)(2,1)}, bf16[4,2,16,4...) while((s32[]{:T(128)}, ...), condition=%wide.wide.region_6.7_spmd, body=%wide.wide.region_3.6_spmd.sunk | while | flops 1090236544 | bytes 46957308 | solution.py:152
  159.5 12.6 %gather_fusion = s32[2048]{0:T(1024)S(1)} fusion(s32[128]{0:T(128)S(1)} %get-tuple-element.348, s32[2048]{0:T(1024)S(1)} %broadcast_clamp_fusion.4), kind=kCustom, calls=%fused_computation.clone.clone.1 | custom fusion | bytes 24576 | tf_op jit(solution)/shard_map/while/body/eval_jaxpr/gather | solution.py:60
  176.2 6.0 %convolution_convert_fusion.7 = bf16[128,16384]{1,0:T(8,128)(2,1)} fusion(bf16[192,16384]{1,0:T(8,128)(2,1)} %get-tuple-element.351, s32[128]{0:T(128)S(1)} %get-tuple-element.304), kind=kOutput, calls=%fused_computation.2.clone.clone.1 | convolution fusion | flops 807428096 | bytes 10486272 | tf_op jit(solution)/shard_map/while/body/eval_jaxpr/dot_general | solution.py:38
  182.2 7.7 %reshape.231 = bf16[128,2,16,4,128]{4,3,2,1,0:T(4,128)(2,1)} reshape(bf16[128,16384]{1,0:T(8,128)(2,1)} %convolution_convert_fusion.7) | data formatting | bytes 8388608 | tf_op jit(solution)/shard_map/while/body/eval_jaxpr/reshape | solution.py:39
  190.0 3.5 %fusion.69 = (bf16[128,1,16,4,128]{4,3,2,1,0:T(4,128)(2,1)S(1)}, bf16[128,1,16,4,128]{4,3,2,1,0:T(4,128)(2,1)S(1)}) fusion(bf16[128,2,16,4,128]{4,3,2,1,0:T(4,128)(2,1)} %reshape.231), kind=kLoop, calls=%fused_computation.95.clone.clone.1 | loop fusion | bytes 8388608 | tf_op jit(solution)/shard_map/while/body/eval_jaxpr/slice | solution.py:72
  199.9 12.6 %gather_fusion = s32[2048]{0:T(1024)S(1)} fusion(s32[128]{0:T(128)S(1)} %get-tuple-element.348, s32[2048]{0:T(1024)S(1)} %broadcast_clamp_fusion.4), kind=kCustom, calls=%fused_computation.clone.clone.1 | custom fusion | bytes 24576 | tf_op jit(solution)/shard_map/while/body/eval_jaxpr/gather | solution.py:60
  216.6 6.0 %convolution_convert_fusion.7 = bf16[128,16384]{1,0:T(8,128)(2,1)} fusion(bf16[192,16384]{1,0:T(8,128)(2,1)} %get-tuple-element.351, s32[128]{0:T(128)S(1)} %get-tuple-element.304), kind=kOutput, calls=%fused_computation.2.clone.clone.1 | convolution fusion | flops 807428096 | bytes 10486272 | tf_op jit(solution)/shard_map/while/body/eval_jaxpr/dot_general | solution.py:38
  222.6 7.7 %reshape.231 = bf16[128,2,16,4,128]{4,3,2,1,0:T(4,128)(2,1)} reshape(bf16[128,16384]{1,0:T(8,128)(2,1)} %convolution_convert_fusion.7) | data formatting | bytes 8388608 | tf_op jit(solution)/shard_map/while/body/eval_jaxpr/reshape | solution.py:39
  230.3 3.5 %fusion.69 = (bf16[128,1,16,4,128]{4,3,2,1,0:T(4,128)(2,1)S(1)}, bf16[128,1,16,4,128]{4,3,2,1,0:T(4,128)(2,1)S(1)}) fusion(bf16[128,2,16,4,128]{4,3,2,1,0:T(4,128)(2,1)} %reshape.231), kind=kLoop, calls=%fused_computation.95.clone.clone.1 | loop fusion | bytes 8388608 | tf_op jit(solution)/shard_map/while/body/eval_jaxpr/slice | solution.py:72
  240.3 12.6 %gather_fusion = s32[2048]{0:T(1024)S(1)} fusion(s32[128]{0:T(128)S(1)} %get-tuple-element.348, s32[2048]{0:T(1024)S(1)} %broadcast_clamp_fusion.4), kind=kCustom, calls=%fused_computation.clone.clone.1 | custom fusion | bytes 24576 | tf_op jit(solution)/shard_map/while/body/eval_jaxpr/gather | solution.py:60
  257.0 6.0 %convolution_convert_fusion.7 = bf16[128,16384]{1,0:T(8,128)(2,1)} fusion(bf16[192,16384]{1,0:T(8,128)(2,1)} %get-tuple-element.351, s32[128]{0:T(128)S(1)} %get-tuple-element.304), kind=kOutput, calls=%fused_computation.2.clone.clone.1 | convolution fusion | flops 807428096 | bytes 10486272 | tf_op jit(solution)/shard_map/while/body/eval_jaxpr/dot_general | solution.py:38
  263.0 7.7 %reshape.231 = bf16[128,2,16,4,128]{4,3,2,1,0:T(4,128)(2,1)} reshape(bf16[128,16384]{1,0:T(8,128)(2,1)} %convolution_convert_fusion.7) | data formatting | bytes 8388608 | tf_op jit(solution)/shard_map/while/body/eval_jaxpr/reshape | solution.py:39
  280.7 12.6 %gather_fusion = s32[2048]{0:T(1024)S(1)} fusion(s32[128]{0:T(128)S(1)} %get-tuple-element.348, s32[2048]{0:T(1024)S(1)} %broadcast_clamp_fusion.4), kind=kCustom, calls=%fused_computation.clone.clone.1 | custom fusion | bytes 24576 | tf_op jit(solution)/shard_map/while/body/eval_jaxpr/gather | solution.py:60
  297.4 6.0 %convolution_convert_fusion.7 = bf16[128,16384]{1,0:T(8,128)(2,1)} fusion(bf16[192,16384]{1,0:T(8,128)(2,1)} %get-tuple-element.351, s32[128]{0:T(128)S(1)} %get-tuple-element.304), kind=kOutput, calls=%fused_computation.2.clone.clone.1 | convolution fusion | flops 807428096 | bytes 10486272 | tf_op jit(solution)/shard_map/while/body/eval_jaxpr/dot_general | solution.py:38
  303.4 7.7 %reshape.231 = bf16[128,2,16,4,128]{4,3,2,1,0:T(4,128)(2,1)} reshape(bf16[128,16384]{1,0:T(8,128)(2,1)} %convolution_convert_fusion.7) | data formatting | bytes 8388608 | tf_op jit(solution)/shard_map/while/body/eval_jaxpr/reshape | solution.py:39
  320.8 3.6 %psum.7 = f32[4,4,1]{1,0,2:T(4,128)S(1)} all-reduce(f32[4,4,1]{1,0,2:T(4,128)S(1)} %bitcast.138), channel_id=1, replica_groups=mesh['rep'=16,'tp'=2] {'tp'}, use_global_device_ids=true, to_apply=%region_8.9 | all-reduce | flops 16 | bytes 128 | tf_op jit(solution)/shard_map/psum | solution.py:166
  (146 shorter events, 64.7 us)
Async XLA Ops:
  0.0 22.9 %copy-start = (bf16[4,4,2,4,128]{4,3,2,1,0:T(4,128)(2,1)S(1)}, bf16[4,4,2,4,128]{4,3,2,1,0:T(4,128)(2,1)}, u32[]{:S(2)}) copy-start(bf16[4,4,2,4,128]{4,3,2,1,0:T(4,128)(2,1)} %param.14) | copy-start | bytes 98308
  0.0 22.9 %copy-start.6 = (bf16[4,2,16,4,128]{4,3,2,1,0:T(4,128)(2,1)S(1)}, bf16[4,2,16,4,128]{4,3,2,1,0:T(4,128)(2,1)}, u32[]{:S(2)}) copy-start(bf16[4,2,16,4,128]{4,3,2,1,0:T(4,128)(2,1)} %param.15) | copy-start | bytes 393220
  11.5 27.0 %all-to-all-start.1 = ((s32[16,8,1]{1,2,0:T(1,128)}), s32[16,8,1]{1,2,0:T(1,128)S(1)}, u32[]{:S(2)}, u32[]{:S(2)}) async-start(s32[16,8,1]{1,2,0:T(1,128)} %bitcast.32), calls=%async_computation.1 | async-start | bytes 16384 | tf_op jit(solution)/shard_map/all_to_all | solution.py:130
  38.5 6.5 %copy-start.2 = (bf16[4,4,64,128]{3,2,1,0:T(8,128)(2,1)S(1)}, bf16[4,4,64,128]{3,2,1,0:T(8,128)(2,1)}, u32[]{:S(2)}) copy-start(bf16[4,4,64,128]{3,2,1,0:T(8,128)(2,1)} %param.13) | copy-start | bytes 786436
  38.5 99.9 %copy-start.1 = (bf16[64,2,16,4,128]{4,3,2,1,0:T(4,128)(2,1)S(1)}, bf16[64,2,16,4,128]{4,3,2,1,0:T(4,128)(2,1)}, u32[]{:S(2)}) copy-start(bf16[64,2,16,4,128]{4,3,2,1,0:T(4,128)(2,1)} %param.16) | copy-start | bytes 6291460
  38.6 99.9 %all-to-all-start = ((bf16[128,2,16,4,128]{4,3,2,1,0:T(4,128)(2,1)}), bf16[128,2,16,4,128]{4,3,2,1,0:T(4,128)(2,1)}, u32[]{:S(2)}, u32[]{:S(2)}) async-start(bf16[128,2,16,4,128]{4,3,2,1,0:T(4,128)(2,1)} %reshape.164), calls=%async_computation | async-start | bytes 8388608 | tf_op jit(solution)/shard_map/all_to_all | solution.py:129
  147.4 11.2 %copy-start.4 = (s32[4]{0:T(128)S(1)}, s32[4]{0:T(128)}, u32[]{:S(2)}) copy-start(s32[4]{0:T(128)} %param.19) | copy-start | bytes 52
  147.4 11.2 %copy-start.5 = (s32[4]{0:T(128)S(1)}, s32[4]{0:T(128)}, u32[]{:S(2)}) copy-start(s32[4]{0:T(128)} %param.22) | copy-start | bytes 52
  147.4 11.2 %copy-start.7 = (s32[4]{0:T(128)S(1)}, s32[4]{0:T(128)}, u32[]{:S(2)}) copy-start(s32[4]{0:T(128)} %param.18) | copy-start | bytes 52
  158.6 165.8 %copy-start.3 = (f32[8192]{0:T(1024)S(1)}, f32[8192]{0:T(1024)}, u32[]{:S(2)}) copy-start(f32[8192]{0:T(1024)} %param.23) | copy-start | bytes 98308
where the time goes:
time: 328 us; the launch traced here: 325 us
  local copies, waits for them, and re-layouts  139 us (42%)
  waiting for transfers between devices  92.1 us (28%)
  matrix products  44.2 us (13%)
  other arithmetic  32.3 us (10%)
  starting transfers between devices  13.1 us (4%)
  blocking collectives  3.57 us (1%)
    all_to_all x1, waiting for transfers between devices, body(): lax.all_to_all(outgoing, 'rep', split_axis=0, concat_axis=0, tiled=True)  92.1 us
    gather x4, local copies, waits for them, and re-layouts, token_validity(): arrival_length[jnp.clip(entry - pool_page_tiles, 0, arrival_length.shape[...  50.5 us
    reshape x5, local copies, waits for them, and re-layouts, pick_rows(): picked.astype(jnp.bfloat16).reshape((selector.shape[0],) + table.shape[1:])  38.6 us
    dot_general x6, matrix products, pick_rows(): jnp.dot(selector.astype(jnp.bfloat16), flat, preferred_element_type=jnp.f...  31.7 us
    slice x8, local copies, waits for them, and re-layouts, attend(): pages[:, 0].reshape(-1, kv_heads, hdim)  20.5 us
    reshape x3, local copies, waits for them, and re-layouts, pick_rows(): flat = table.reshape(table.shape[0], -1)  14.5 us
    dot_general x4, matrix products, attend(): jnp.einsum('skgd,lkd->skgl', grouped, keys, preferred_element_type=jnp.fl...  9.91 us
    concatenate x1, other arithmetic, body(): extended = jnp.concatenate([cache_block_store, arrived], 0)  8.9 us
  transfers between devices with their start and end apart: 2, of which 1 were waited for; matrix products, arithmetic and copies ran while one was open for 7% of the time, Pallas kernels for 0%

commit v1 on v0

v1 whole, which is shorter than its diff:
```python
import functools
import math

import jax
import jax.numpy as jnp
from jax import lax
from jax.experimental import pallas as pl
from jax.experimental.pallas import tpu as pltpu
from jax.sharding import PartitionSpec as P

NEG = -1e30
LOG2E = 1.4426950408889634
VMEM_LIMIT = 50 * 1024 * 1024


def pack_kernel(cap, sender, target, lengths, tiles, out, held):
    replicas = out.shape[0]
    pool = tiles.shape[0] - lengths.shape[0]
    parts, kv, page, hdim = tiles.shape[1:]
    for d in range(replicas):
        held[d] = 0
    lane = lax.broadcasted_iota(jnp.int32, (page, hdim), 1)
    out[...] = jnp.zeros_like(out)

    def place(e, carry):
        d = target[e, 0]
        rank = held[d]
        held[d] = rank + 1
        source = sender[e]
        for c in range(parts):
            for k in range(kv):
                out[d, (c * kv + k) * cap + rank] = tiles[source, c, k]
        from_tail = source >= pool
        length = jnp.where(from_tail, lengths[jnp.maximum(source - pool, 0)], page)
        inside = (lane >= rank * page) & (lane < rank * page + length)
        mask = out[d, parts * kv * cap]
        out[d, parts * kv * cap] = jnp.where(inside, 1.0, mask.astype(jnp.float32)).astype(mask.dtype)
        return carry

    lax.fori_loop(0, sender.shape[0], place, 0)


def pack(tiles, sender, target, lengths, replicas, cap):
    _, parts, kv, page, hdim = tiles.shape
    smem = pl.BlockSpec(memory_space=pltpu.SMEM)
    vmem = pl.BlockSpec(memory_space=pltpu.VMEM)
    return pl.pallas_call(
        functools.partial(pack_kernel, cap),
        out_shape=jax.ShapeDtypeStruct((replicas, parts * kv * cap + 1, page, hdim), tiles.dtype),
        in_specs=[smem, smem, smem, vmem],
        out_specs=vmem,
        scratch_shapes=[pltpu.SMEM((replicas,), jnp.int32)],
        compiler_params=pltpu.CompilerParams(vmem_limit_bytes=VMEM_LIMIT),
        name="pack",
    )(sender, target, lengths, tiles)


def counts_of(table, history, first, pages, page):
    requests, entries = table.shape
    offset = lax.broadcasted_iota(jnp.int32, (page, entries), 0)
    position = lax.broadcasted_iota(jnp.int32, (page, entries), 1) * page + offset
    named = lax.broadcasted_iota(jnp.int32, (pages, entries), 0) + first
    per_page = []
    for g in range(requests):
        inside = jnp.where(position < history[g], 1.0, 0.0).astype(jnp.bfloat16)
        hit = jnp.where(table[g : g + 1, :] == named, 1.0, 0.0).astype(jnp.bfloat16)
        per_page.append(
            lax.dot_general(inside, hit, (((1,), (1,)), ((), ())), preferred_element_type=jnp.float32)
        )
    tokens = pages * page
    spread = (
        lax.broadcasted_iota(jnp.int32, (pages, tokens), 1) // page
        == lax.broadcasted_iota(jnp.int32, (pages, tokens), 0)
    )
    wide = jnp.dot(
        jnp.concatenate(per_page, 0).astype(jnp.bfloat16),
        jnp.where(spread, 1.0, 0.0).astype(jnp.bfloat16),
        preferred_element_type=jnp.float32,
    )
    own = (
        lax.broadcasted_iota(jnp.int32, (page, tokens), 1) % page
        == lax.broadcasted_iota(jnp.int32, (page, tokens), 0)
    )
    return [
        jnp.sum(jnp.where(own, wide[g * page : (g + 1) * page], 0.0), axis=0, keepdims=True)
        for g in range(requests)
    ]


def bias_of(count):
    return jnp.where(count > 0.0, jnp.log2(jnp.maximum(count, 1.0)), NEG)


def head_scores(query, keys, bias):
    rows, hdim = query.shape
    scores = lax.dot_general(query, keys, (((1,), (1,)), ((), ())), preferred_element_type=jnp.float32)
    groups = bias.shape[0]
    scores = scores.reshape(groups, rows // groups, -1) * (LOG2E / math.sqrt(hdim)) + bias[:, None, :]
    return scores.reshape(rows, -1)


def pool_kernel(history, fill, table, query, tiles, mixed, top, total, bias):
    steps, requests, heads, hdim = query.shape
    all_pages, _, kv, page, _ = tiles.shape
    pool = all_pages - requests
    counts = counts_of(table, history, 0, pool, page)
    tail = lax.broadcasted_iota(jnp.int32, (1, requests * page), 1)
    for t in range(steps):
        for g in range(requests):
            row = t * requests + g
            bias[row : row + 1, : pool * page] = bias_of(counts[g])
            seen = (tail // page == g) & (tail % page < fill[g] + t + 1)
            bias[row : row + 1, pool * page :] = jnp.where(seen, 0.0, NEG)
    group = heads // kv
    rows = steps * requests * group

    def one_head(k, carry):
        q = query[:, :, pl.ds(k * group, group), :].reshape(rows, hdim)
        keys = tiles[:, 0, k].reshape(all_pages * page, hdim)
        values = tiles[:, 1, k].reshape(all_pages * page, hdim)
        scores = head_scores(q, keys, bias[...])
        best = jnp.max(scores, axis=-1, keepdims=True)
        probs = jnp.exp2(scores - best)
        total[k] = jnp.sum(probs, axis=-1, keepdims=True)
        top[k] = best
        mixed[k] = jnp.dot(probs.astype(jnp.bfloat16), values, preferred_element_type=jnp.float32)
        return carry

    lax.fori_loop(0, kv, one_head, 0)


def attend_pool(query, tiles, table, history, fill):
    steps, requests, heads, hdim = query.shape
    all_pages, _, kv, page, _ = tiles.shape
    rows = steps * requests * heads // kv
    smem = pl.BlockSpec(memory_space=pltpu.SMEM)
    vmem = pl.BlockSpec(memory_space=pltpu.VMEM)
    one = jax.ShapeDtypeStruct((kv, rows, 1), jnp.float32)
    flops = 4 * kv * rows * all_pages * page * hdim
    return pl.pallas_call(
        pool_kernel,
        out_shape=(jax.ShapeDtypeStruct((kv, rows, hdim), jnp.float32), one, one),
        in_specs=[smem, smem, vmem, vmem, vmem],
        out_specs=(vmem, vmem, vmem),
        scratch_shapes=[pltpu.VMEM((steps * requests, all_pages * page), jnp.float32)],
        compiler_params=pltpu.CompilerParams(vmem_limit_bytes=VMEM_LIMIT),
        cost_estimate=pl.CostEstimate(flops=8 * flops, bytes_accessed=8 << 20, transcendentals=0),
        name="attend_pool",
    )(history, fill, table, query, tiles)


def arrival_kernel(cap, pool, history, switch, table, query, arrived, mixed0, top0, total0, attn, square, bias):
    steps, requests, heads, hdim = query.shape
    replicas = arrived.shape[0]
    kv, page = mixed0.shape[0], arrived.shape[2]
    tokens = replicas * cap * page
    counts = counts_of(table, history, pool, replicas * cap, page)
    here = arrived[:, 2 * kv * cap, 0, :]
    width = cap * page
    repeat = (
        lax.broadcasted_iota(jnp.int32, (hdim, tokens), 1) % width
        == lax.broadcasted_iota(jnp.int32, (hdim, tokens), 0)
    )
    spread = jnp.dot(here, jnp.where(repeat, 1.0, 0.0).astype(jnp.bfloat16), preferred_element_type=jnp.float32)
    mine = (
        lax.broadcasted_iota(jnp.int32, (replicas, tokens), 1) // width
        == lax.broadcasted_iota(jnp.int32, (replicas, tokens), 0)
    )
    filled = jnp.sum(jnp.where(mine, spread, 0.0), axis=0, keepdims=True)
    for g in range(requests):
        usable = bias_of(counts[g] * filled)
        for t in range(steps):
            row = t * requests + g
            bias[row : row + 1, :] = jnp.where(t >= switch[g], usable, NEG)
    group = heads // kv
    rows = steps * requests * group
    square[...] = jnp.zeros_like(square)

    def one_head(k, carry):
        q = query[:, :, pl.ds(k * group, group), :].reshape(rows, hdim)
        keys = arrived[:, pl.ds(k * cap, cap)].reshape(tokens, hdim)
        values = arrived[:, pl.ds((kv + k) * cap, cap)].reshape(tokens, hdim)
        scores = head_scores(q, keys, bias[...])
        before = top0[k]
        best = jnp.maximum(jnp.max(scores, axis=-1, keepdims=True), before)
        probs = jnp.exp2(scores - best)
        kept = jnp.exp2(before - best)
        total = jnp.sum(probs, axis=-1, keepdims=True) + total0[k] * kept
        out = jnp.dot(probs.astype(jnp.bfloat16), values, preferred_element_type=jnp.float32)
        out = ((out + mixed0[k] * kept) / total).astype(jnp.bfloat16)
        attn[:, :, pl.ds(k * group, group), :] = out.reshape(steps, requests, group, hdim)
        wide = out.astype(jnp.float32)
        square[...] += jnp.sum((wide * wide).reshape(steps * requests, group, hdim), axis=1)
        return carry

    lax.fori_loop(0, kv, one_head, 0)


def attend_arrivals(query, arrived, table, history, switch, mixed, top, total, cap, pool):
    steps, requests, heads, hdim = query.shape
    replicas, _, page, _ = arrived.shape
    smem = pl.BlockSpec(memory_space=pltpu.SMEM)
    vmem = pl.BlockSpec(memory_space=pltpu.VMEM)
    return pl.pallas_call(
        functools.partial(arrival_kernel, cap, pool),
        out_shape=(
            jax.ShapeDtypeStruct(query.shape, jnp.bfloat16),
            jax.ShapeDtypeStruct((steps * requests, hdim), jnp.float32),
        ),
        in_specs=[smem, smem] + [vmem] * 6,
        out_specs=(vmem, vmem),
        scratch_shapes=[pltpu.VMEM((steps * requests, replicas * cap * page), jnp.float32)],
        compiler_params=pltpu.CompilerParams(vmem_limit_bytes=VMEM_LIMIT),
        name="attend_arrivals",
    )(history, switch, table, query, arrived, mixed, top, total)


def filled_tail(unfinished, fresh, fill):
    offset = jnp.arange(unfinished.shape[2], dtype=jnp.int32)[None, None, :, None, None]
    out = unfinished
    for s in range(fresh.shape[0]):
        out = jnp.where(offset == fill[:, None, None, None, None] + s, fresh[s][:, :, None], out)
    return out


def body(query, fresh, unfinished, store, table, history, fill, sender, target, switch, gain):
    replicas = lax.axis_size("rep")
    steps, requests, heads, hdim = query.shape
    pool = store.shape[0]
    cap = max(2, 2 * sender.shape[0] // replicas)
    tiles = jnp.concatenate([store, filled_tail(unfinished, fresh, fill)], 0)
    tiles = jnp.transpose(tiles, (0, 1, 3, 2, 4))
    outgoing = pack(tiles, sender, target, fill + switch, replicas, cap)
    arrived = lax.all_to_all(outgoing, "rep", split_axis=0, concat_axis=0, tiled=True)
    mixed, top, total = attend_pool(query, tiles, table, history, fill)
    attn, square = attend_arrivals(
        query, arrived, table, history, switch, mixed, top, total, cap, pool
    )
    square = lax.psum(jnp.sum(square, axis=-1).reshape(steps, requests, 1), "tp")
    width = heads * hdim * lax.axis_size("tp")
    wide = attn.reshape(steps, requests, heads * hdim).astype(jnp.float32)
    return (wide * lax.rsqrt(square / width + 1e-05) * gain).astype(jnp.bfloat16)


def solution(mesh):
    placed = (
        P(None, "rep", "tp", None),
        P(None, "rep", None, "tp", None),
        P("rep", None, None, "tp", None),
        P("rep", None, None, "tp", None),
        P("rep", None),
        P("rep"),
        P("rep"),
        P("rep"),
        P("rep", None),
        P("rep"),
        P("tp"),
    )
    return jax.shard_map(
        body, mesh=mesh, in_specs=placed, out_specs=P(None, "rep", "tp"), check_vma=False
    )
```

time: 328 us -> 128 us (0.39)
  local copies, waits for them, and re-layouts: 139 us -> 6.42 us
  matrix products: 44.2 us -> 0 us
  other arithmetic: 32.3 us -> 2.83 us
  Pallas kernels: 0 us -> 16.8 us
  starting transfers between devices: 13.1 us -> 6.72 us
    gather x6 -> x0, local copies, waits for them, and re-layouts: 53.4 us -> none  [the longest x4 50.5 us: token_validity(): arrival_length[jnp.clip(entry - pool_page_tiles, 0, arrival_length.shape[...]
    reshape x8 -> x1, local copies, waits for them, and re-layouts: 53.2 us -> 0.08 us  [body(): jnp.sum(square, axis=-1).reshape(steps, requests, 1)]
    dot_general x15 -> x0, matrix products: 44.2 us -> none  [the longest x6 31.7 us: pick_rows(): jnp.dot(selector.astype(jnp.bfloat16), flat, preferred_element_type=jnp.f...]
    slice x12 -> x0, local copies, waits for them, and re-layouts: 21.7 us -> none  [the longest x8 20.5 us: attend(): pages[:, 0].reshape(-1, kv_heads, hdim)]
    pallas_call x0 -> x3, Pallas kernels: none -> 16.8 us  [the longest x1 7.92 us: attend_arrivals(): pl.pallas_call(functools.partial(arrival_kernel, cap, pool), out_shape=(j...]
    concatenate x5 -> x0, other arithmetic: 8.96 us -> none  [the longest x1 8.9 us: body(): extended = jnp.concatenate([cache_block_store, arrived], 0)]
    dynamic_slice x16 -> x0, local copies, waits for them, and re-layouts: 7.42 us -> none  [body(): lax.map(one_request, (jnp.transpose(lookup_vectors, (1, 0, 2, 3)), sequen...]
    all_to_all x1 -> x0, starting transfers between devices: 6.58 us -> none  [body(): lax.all_to_all(out_len, 'rep', split_axis=0, concat_axis=0, tiled=True)]
  transfers between devices with their start and end apart: 2 -> 1, of which waited for: 1 -> 1; matrix products, arithmetic and copies ran while one was open for 7% -> 0% of each run, Pallas kernels for 0% -> 3%
where the time goes in v1:
time: 128 us; the launch traced here: 127 us
  waiting for transfers between devices  90.8 us (71%)
  Pallas kernels  16.8 us (13%)
  starting transfers between devices  6.72 us (5%)
  local copies, waits for them, and re-layouts  6.42 us (5%)
  blocking collectives  3.56 us (3%)
  other arithmetic  2.83 us (2%)
    all_to_all x1, waiting for transfers between devices, body(): lax.all_to_all(outgoing, 'rep', split_axis=0, concat_axis=0, tiled=True)  90.8 us
    pallas_call x1, Pallas kernels, attend_arrivals(): pl.pallas_call(functools.partial(arrival_kernel, cap, pool), out_shape=(j...  7.92 us
    all_to_all x1, starting transfers between devices, body(): lax.all_to_all(outgoing, 'rep', split_axis=0, concat_axis=0, tiled=True)  6.72 us
    unnamed x22, local copies, waits for them, and re-layouts  5.37 us
    pallas_call x1, Pallas kernels, pack(): pl.pallas_call(functools.partial(pack_kernel, cap), out_shape=jax.ShapeDt...  4.6 us
    pallas_call x1, Pallas kernels, attend_pool(): pl.pallas_call(pool_kernel, out_shape=(jax.ShapeDtypeStruct((kv, rows, hd...  4.24 us
    psum x1, blocking collectives, body(): lax.psum(jnp.sum(square, axis=-1).reshape(steps, requests, 1), 'tp')  3.56 us
  transfers between devices with their start and end apart: 1, of which 1 were waited for; matrix products, arithmetic and copies ran while one was open for 0% of the time, Pallas kernels for 3%

profile of v1, /device:TPU:15, one launch (start us, length us, event | category | flops | bytes accessed | tf_op | source)
XLA Modules:
  0.0 127.2 jit_solution(18058689541802920597)
XLA Ops:
  0.0 0.7 broadcast_add_fusion.2
  0.7 0.7 iota_compare_fusion
  1.4 0.7 copy.14.target
  2.2 0.8 slice_bitcast_fusion.3
  2.9 2.3 %copy.13 = bf16[64,2,16,4,128]{4,2,3,1,0:T(8,128)(2,1)S(1)} copy(bf16[64,2,16,4,128]{4,3,2,1,0:T(4,128)(2,1)} %param.14) | data formatting | bytes 4194304 | tf_op args[3]
  5.2 0.1 iota_compare_fusion.1
  5.3 0.0 copy-done.8
  5.3 0.1 fusion.2
  5.4 0.0 copy-start.7
  5.4 0.2 maximum_bitcast_fusion.tiles
  5.6 0.4 copy-done.7
  6.1 4.6 %pack.1 = bf16[16,65,16,128]{3,2,1,0:T(8,128)(2,1)} custom-call(s32[64]{0:T(128)S(1)} %copy-done.7, s32[64,1]{1,0:T(8,128)S(1)} %copy.14.target, s32[4]{0:T(128)S(1)} %get-tuple-element.22.lengths, bf16[68,2,4,16,128]{4,3,2,1,0:T(8,128)(2,1)S(1)} %maximum_bitcast_fusion.tiles), custom_call_target="tpu_custom_call" | custom-call | tf_op jit(solution)/shard_map/pack/pallas_call | solution.py:47
  10.7 6.7 %all-to-all-start = ((bf16[16,65,16,128]{3,2,1,0:T(8,128)(2,1)}), bf16[16,65,16,128]{3,2,1,0:T(8,128)(2,1)}, u32[]{:S(2)}, u32[]{:S(2)}) async-start(bf16[16,65,16,128]{3,2,1,0:T(8,128)(2,1)} %pack.1), calls=%async_computation | async-start | bytes 8519680 | tf_op jit(solution)/shard_map/all_to_all | solution.py:234
  17.4 0.0 copy-start.4
  17.5 4.2 %attend_pool.1 = (f32[4,256,128]{2,1,0:T(8,128)S(1)}, f32[4,256,1]{2,1,0:T(8,128)S(1)}, f32[4,256,1]{2,1,0:T(8,128)S(1)}) custom-call(s32[4]{0:T(128)S(1)} %copy-done.6, s32[4]{0:T(128)S(1)} %copy-done.5, s32[4,128]{1,0:T(4,128)S(1)} %copy-done.3, bf16[4,4,64,128]{3,2,1,0:T(8,128)(2,1)S(1)} %copy-done.2, ...), custom_call_target="tpu_custom_call" | custom-call | flops 4563402752 | bytes 8388608 | tf_op jit(solution)/shard_map/attend_pool/pallas_call | solution.py:140
  21.7 0.8 copy-done
  22.6 90.8 %all-to-all-done.arrived = bf16[16,65,16,128]{3,2,1,0:T(8,128)(2,1)} async-done(((bf16[16,65,16,128]{3,2,1,0:T(8,128)(2,1)}), bf16[16,65,16,128]{3,2,1,0:T(8,128)(2,1)}, u32[]{:S(2)}, u32[]{:S(2)}) %all-to-all-start) | async-done | bytes 4259872 | tf_op jit(solution)/shard_map/all_to_all | solution.py:234
  113.4 1.0 copy-done.1
  114.4 7.9 %attend_arrivals.1 = (bf16[4,4,64,128]{3,2,1,0:T(8,128)(2,1)S(1)}, f32[16,128]{1,0:T(8,128)S(1)}) custom-call(s32[4]{0:T(128)S(1)} %copy-done.6, s32[4]{0:T(128)S(1)} %copy-done.4, s32[4,128]{1,0:T(4,128)S(1)} %copy-done.3, bf16[4,4,64,128]{3,2,1,0:T(8,128)(2,1)S(1)} %copy-done.2, bf16[16,65,16,128]{3,2,1,0:T(8,128)(2,1)} %all-to-all-done.arrived, ...), custom_call_target="tpu_custom_call" | custom-call | tf_op jit(solution)/shard_map/attend_arrivals/pallas_call | solution.py:204
  122.3 0.1 reduce_sum.9
  122.4 0.1 reshape.108
  122.5 3.6 %psum.7 = f32[4,4,1]{1,0,2:T(4,128)S(1)} all-reduce(f32[4,4,1]{1,0,2:T(4,128)S(1)} %reshape.108), channel_id=1, replica_groups=mesh['rep'=16,'tp'=2] {'tp'}, use_global_device_ids=true, to_apply=%region_1.2 | all-reduce | flops 16 | bytes 128 | tf_op jit(solution)/shard_map/psum | solution.py:239
  126.1 0.2 reshape.109
  126.3 0.9 multiply_convert_fusion
  (15 shorter events, 0.0 us)
Async XLA Ops:
  0.0 5.3 %copy-start.8 = (bf16[4,2,16,4,128]{4,3,2,1,0:T(4,128)(2,1)S(1)}, bf16[4,2,16,4,128]{4,3,2,1,0:T(4,128)(2,1)}, u32[]{:S(2)}) copy-start(bf16[4,2,16,4,128]{4,3,2,1,0:T(4,128)(2,1)} %param.13) | copy-start | bytes 393220
  5.4 0.7 copy-start.7
  10.7 6.7 %copy-start.2 = (bf16[4,4,64,128]{3,2,1,0:T(8,128)(2,1)S(1)}, bf16[4,4,64,128]{3,2,1,0:T(8,128)(2,1)}, u32[]{:S(2)}) copy-start(bf16[4,4,64,128]{3,2,1,0:T(8,128)(2,1)} %query.3) | copy-start | bytes 786436
  10.7 6.7 %copy-start.3 = (s32[4,128]{1,0:T(4,128)S(1)}, s32[4,128]{1,0:T(4,128)}, u32[]{:S(2)}) copy-start(s32[4,128]{1,0:T(4,128)} %table.3) | copy-start | bytes 6148
  10.7 6.8 %copy-start.5 = (s32[4]{0:T(128)S(1)}, s32[4]{0:T(128)}, u32[]{:S(2)}) copy-start(s32[4]{0:T(128)} %fill.1) | copy-start | bytes 52
  10.7 6.8 %copy-start.6 = (s32[4]{0:T(128)S(1)}, s32[4]{0:T(128)}, u32[]{:S(2)}) copy-start(s32[4]{0:T(128)} %history.3) | copy-start | bytes 52
  10.7 102.7 %all-to-all-start = ((bf16[16,65,16,128]{3,2,1,0:T(8,128)(2,1)}), bf16[16,65,16,128]{3,2,1,0:T(8,128)(2,1)}, u32[]{:S(2)}, u32[]{:S(2)}) async-start(bf16[16,65,16,128]{3,2,1,0:T(8,128)(2,1)} %pack.1), calls=%async_computation | async-start | bytes 8519680 | tf_op jit(solution)/shard_map/all_to_all | solution.py:234
  17.4 95.9 %copy-start.4 = (s32[4]{0:T(128)S(1)}, s32[4]{0:T(128)}, u32[]{:S(2)}) copy-start(s32[4]{0:T(128)} %switch.1) | copy-start | bytes 52
  21.7 0.9 copy-start
  113.4 1.0 copy-start.1
  114.4 11.9 %copy-start.9 = (f32[8192]{0:T(1024)S(1)}, f32[8192]{0:T(1024)}, u32[]{:S(2)}) copy-start(f32[8192]{0:T(1024)} %param.21) | copy-start | bytes 98308

commit v2 on v1

v2 whole, which is shorter than its diff:
```python
import functools
import math

import jax
import jax.numpy as jnp
from jax import lax
from jax.experimental import pallas as pl
from jax.experimental.pallas import tpu as pltpu
from jax.sharding import PartitionSpec as P

NEG = -1e30
LOG2E = 1.4426950408889634
VMEM_LIMIT = 50 * 1024 * 1024


def counts_of(table, history, first, pages, page):
    requests, entries = table.shape
    offset = lax.broadcasted_iota(jnp.int32, (page, entries), 0)
    position = lax.broadcasted_iota(jnp.int32, (page, entries), 1) * page + offset
    named = lax.broadcasted_iota(jnp.int32, (pages, entries), 0) + first
    per_page = []
    for g in range(requests):
        inside = jnp.where(position < history[g], 1.0, 0.0).astype(jnp.bfloat16)
        hit = jnp.where(table[g : g + 1, :] == named, 1.0, 0.0).astype(jnp.bfloat16)
        per_page.append(
            lax.dot_general(inside, hit, (((1,), (1,)), ((), ())), preferred_element_type=jnp.float32)
        )
    tokens = pages * page
    spread = (
        lax.broadcasted_iota(jnp.int32, (pages, tokens), 1) // page
        == lax.broadcasted_iota(jnp.int32, (pages, tokens), 0)
    )
    wide = jnp.dot(
        jnp.concatenate(per_page, 0).astype(jnp.bfloat16),
        jnp.where(spread, 1.0, 0.0).astype(jnp.bfloat16),
        preferred_element_type=jnp.float32,
    )
    own = (
        lax.broadcasted_iota(jnp.int32, (page, tokens), 1) % page
        == lax.broadcasted_iota(jnp.int32, (page, tokens), 0)
    )
    return [
        jnp.sum(jnp.where(own, wide[g * page : (g + 1) * page], 0.0), axis=0, keepdims=True)
        for g in range(requests)
    ]


def bias_of(count):
    return jnp.where(count > 0.0, jnp.log2(jnp.maximum(count, 1.0)), NEG)


def head_scores(query, keys, bias):
    rows, hdim = query.shape
    scores = lax.dot_general(query, keys, (((1,), (1,)), ((), ())), preferred_element_type=jnp.float32)
    groups = bias.shape[0]
    scores = scores.reshape(groups, rows // groups, -1) * (LOG2E / math.sqrt(hdim)) + bias[:, None, :]
    return scores.reshape(rows, -1)


def pack_kernel(cap, plane, sender, target, history, fill, switch, tiles, table, out, count, bias, held):
    replicas = out.shape[0]
    requests = fill.shape[0]
    pool = tiles.shape[0] - requests
    parts, kv, page, hdim = tiles.shape[1:]
    steps = bias.shape[0] // requests
    for d in range(replicas):
        held[d] = 0
    lane = lax.broadcasted_iota(jnp.int32, (page, hdim), 1)
    out[...] = jnp.zeros_like(out)

    def place(e, carry):
        d = target[e, 0]
        rank = held[d]
        held[d] = rank + 1
        source = sender[e]
        for c in range(parts):
            for k in range(kv):
                out[d, (c * kv + k) * cap + rank] = tiles[source, c, k]
        owner = jnp.maximum(source - pool, 0)
        length = jnp.where(source >= pool, fill[owner] + switch[owner], page)
        inside = (lane >= rank * page) & (lane < rank * page + length)
        mask = out[d, parts * kv * cap]
        out[d, parts * kv * cap] = jnp.where(inside, 1.0, mask.astype(jnp.float32)).astype(mask.dtype)
        return carry

    lax.fori_loop(0, sender.shape[0], place, 0)
    own = counts_of(table, history, 0, pool, page)
    tail = lax.broadcasted_iota(jnp.int32, (1, requests * page), 1)
    arrivals = counts_of(table, history, pool, replicas * cap, page)
    width = plane * cap * page
    for t in range(steps):
        for g in range(requests):
            row = t * requests + g
            bias[row : row + 1, : pool * page] = bias_of(own[g])
            seen = (tail // page == g) & (tail % page < fill[g] + t + 1)
            bias[row : row + 1, pool * page :] = jnp.where(seen, 0.0, NEG)
    for line in range(replicas // plane):
        rows = []
        for t in range(steps):
            for g in range(requests):
                part = arrivals[g][:, line * width : (line + 1) * width]
                rows.append(jnp.where(t >= switch[g], part, 0.0))
        count[line] = jnp.concatenate(rows, 0).astype(count.dtype)


def pack(tiles, sender, target, table, history, fill, switch, steps, replicas, cap, plane):
    pages, parts, kv, page, hdim = tiles.shape
    requests = fill.shape[0]
    smem = pl.BlockSpec(memory_space=pltpu.SMEM)
    vmem = pl.BlockSpec(memory_space=pltpu.VMEM)
    return pl.pallas_call(
        functools.partial(pack_kernel, cap, plane),
        out_shape=(
            jax.ShapeDtypeStruct((replicas, parts * kv * cap + 1, page, hdim), tiles.dtype),
            jax.ShapeDtypeStruct((replicas // plane, steps * requests, plane * cap * page), jnp.bfloat16),
            jax.ShapeDtypeStruct((steps * requests, pages * page), jnp.float32),
        ),
        in_specs=[smem] * 5 + [vmem] * 2,
        out_specs=(vmem, vmem, vmem),
        scratch_shapes=[pltpu.SMEM((replicas,), jnp.int32)],
        compiler_params=pltpu.CompilerParams(vmem_limit_bytes=VMEM_LIMIT),
        name="pack",
    )(sender, target, history, fill, switch, tiles, table)


def partial(query, keys, values, bias):
    scores = head_scores(query, keys, bias)
    best = jnp.max(scores, axis=-1, keepdims=True)
    probs = jnp.exp2(scores - best)
    total = jnp.sum(probs, axis=-1, keepdims=True)
    return jnp.dot(probs.astype(jnp.bfloat16), values, preferred_element_type=jnp.float32), best, total


def diagonal(size):
    return lax.broadcasted_iota(jnp.int32, (size, size), 0) == lax.broadcasted_iota(jnp.int32, (size, size), 1)


def attend_kernel(
    cap, plane, lines, total_width,
    query, count, bias, gain, tiles, outgoing,
    out,
    arrived, asked, asked_count, answer, answer_log, given, given_log, mixed, top, total, attn, square,
    own_sem, tile_send, tile_recv, ask_send, ask_recv, count_send, count_recv,
    answer_send, answer_recv, log_send, log_recv, square_sem,
):
    steps, requests, heads, hdim = query.shape
    all_pages, _, kv, page, _ = tiles.shape
    group = heads // kv
    groups = steps * requests
    rows = groups * group
    tokens = plane * cap * page
    me = lax.axis_index("rep")
    core = lax.axis_index("tp")
    line, place = lax.div(me, plane), lax.rem(me, plane)

    def peer(a_line, a_place):
        return {"rep": a_line * plane + a_place}

    def send(source, target, send_sem, recv_sem, device):
        return pltpu.make_async_remote_copy(
            src_ref=source, dst_ref=target, send_sem=send_sem, recv_sem=recv_sem,
            device_id=device, device_id_type=pl.DeviceIdType.MESH,
        )

    def line_at(step):
        return lax.rem(line + step, lines)

    def line_back(step):
        return lax.rem(line + lines - step, lines)

    def place_at(step):
        return lax.rem(place + step, plane)

    barrier = pltpu.get_barrier_semaphore()
    for j in range(1, lines):
        pl.semaphore_signal(barrier, inc=1, device_id=peer(line_at(j), place), device_id_type=pl.DeviceIdType.MESH)
    for i in range(1, plane):
        pl.semaphore_signal(barrier, inc=1, device_id=peer(line, place_at(i)), device_id_type=pl.DeviceIdType.MESH)
    pl.semaphore_signal(barrier, inc=1, device_id={"tp": 1 - core}, device_id_type=pl.DeviceIdType.MESH)
    pl.semaphore_wait(barrier, lines + plane - 1)

    def ask(j):
        to = line_at(j)
        return (
            send(query, asked.at[line], ask_send.at[to], ask_recv.at[line], peer(to, place)),
            send(count.at[to], asked_count.at[line], count_send.at[to], count_recv.at[line], peer(to, place)),
        )

    def ship(j, i):
        to = line_at(j)
        mate = place_at(i)
        return send(
            outgoing.at[to * plane + mate], arrived.at[to, place],
            tile_send.at[to, mate], tile_recv.at[to, place], peer(line, mate),
        )

    def keep(j):
        to = line_at(j)
        return pltpu.make_async_copy(outgoing.at[to * plane + place], arrived.at[to, place], own_sem.at[to])

    def reply(j):
        to = line_at(j)
        return (
            send(answer.at[to], given.at[line], answer_send.at[to], answer_recv.at[line], peer(to, place)),
            send(answer_log.at[to], given_log.at[line], log_send.at[to], log_recv.at[line], peer(to, place)),
        )

    for j in range(1, lines + 1):
        for i in range(1, plane):
            ship(j, i).start()
        keep(j).start()
        if j < lines:
            for copy in ask(lines - j):
                copy.start()

    def pool_head(k, carry):
        q = query[:, :, pl.ds(k * group, group), :].reshape(rows, hdim)
        keys = tiles[:, 0, k].reshape(all_pages * page, hdim)
        values = tiles[:, 1, k].reshape(all_pages * page, hdim)
        mixed[k], top[k], total[k] = partial(q, keys, values, bias[...])
        return carry

    lax.fori_loop(0, kv, pool_head, 0)

    width = cap * page
    repeat = (
        lax.broadcasted_iota(jnp.int32, (hdim, tokens), 1) % width
        == lax.broadcasted_iota(jnp.int32, (hdim, tokens), 0)
    )
    repeat = jnp.where(repeat, 1.0, 0.0).astype(jnp.bfloat16)
    mine = (
        lax.broadcasted_iota(jnp.int32, (plane, tokens), 1) // width
        == lax.broadcasted_iota(jnp.int32, (plane, tokens), 0)
    )
    eye = diagonal(rows)

    def filled(to):
        here = arrived[to, :, 2 * kv * cap, 0, :]
        spread = jnp.dot(here, repeat, preferred_element_type=jnp.float32)
        return jnp.sum(jnp.where(mine, spread, 0.0), axis=0, keepdims=True)

    def arrivals(to, k):
        keys = arrived[to, :, pl.ds(k * cap, cap)].reshape(tokens, hdim)
        values = arrived[to, :, pl.ds((kv + k) * cap, cap)].reshape(tokens, hdim)
        return keys, values

    for j in range(1, lines):
        to = line_at(j)
        for i in range(1, plane):
            source = place_at(i)
            send(
                outgoing.at[0], arrived.at[to, source], tile_send.at[to, source], tile_recv.at[to, source],
                peer(line, source),
            ).wait_recv()
        keep(j).wait()
        send(query, asked.at[to], ask_send.at[to], ask_recv.at[to], peer(to, place)).wait_recv()
        send(
            count.at[to], asked_count.at[to], count_send.at[to], count_recv.at[to], peer(to, place)
        ).wait_recv()
        set_bias = bias_of(asked_count[to].astype(jnp.float32) * filled(to))

        def set_head(k, carry):
            q = asked[to, :, :, pl.ds(k * group, group), :].reshape(rows, hdim)
            keys, values = arrivals(to, k)
            part, best, amount = partial(q, keys, values, set_bias)
            answer[to, k] = (part / amount).astype(jnp.bfloat16)
            log = best + jnp.log2(amount)
            answer_log[to, k] = jnp.sum(jnp.where(eye, log, 0.0), axis=0, keepdims=True)
            return carry

        lax.fori_loop(0, kv, set_head, 0)
        for copy in reply(j):
            copy.start()

    for i in range(1, plane):
        source = place_at(i)
        send(
            outgoing.at[0], arrived.at[line, source], tile_send.at[line, source], tile_recv.at[line, source],
            peer(line, source),
        ).wait_recv()
    keep(lines).wait()
    last_bias = bias_of(count[line].astype(jnp.float32) * filled(line))

    def last_head(k, carry):
        q = query[:, :, pl.ds(k * group, group), :].reshape(rows, hdim)
        keys, values = arrivals(line, k)
        part, best, amount = partial(q, keys, values, last_bias)
        high = jnp.maximum(best, top[k])
        fresh, old = jnp.exp2(best - high), jnp.exp2(top[k] - high)
        mixed[k] = part * fresh + mixed[k] * old
        total[k] = amount * fresh + total[k] * old
        top[k] = high
        return carry

    lax.fori_loop(0, kv, last_head, 0)

    for j in range(1, lines):
        to = line_at(j)
        send(answer.at[to], given.at[to], answer_send.at[to], answer_recv.at[to], peer(to, place)).wait_recv()
        send(answer_log.at[to], given_log.at[to], log_send.at[to], log_recv.at[to], peer(to, place)).wait_recv()

    square[0] = jnp.zeros_like(square[0])

    def merge_head(k, carry):
        logs = []
        high = top[k]
        for j in range(1, lines):
            log = jnp.sum(jnp.where(eye, given_log[line_at(j), k], 0.0), axis=1, keepdims=True)
            logs.append(log)
            high = jnp.maximum(high, log)
        old = jnp.exp2(top[k] - high)
        whole = mixed[k] * old
        amount = total[k] * old
        for j in range(1, lines):
            share = jnp.exp2(logs[j - 1] - high)
            whole = whole + given[line_at(j), k].astype(jnp.float32) * share
            amount = amount + share
        result = (whole / amount).astype(jnp.bfloat16)
        attn[:, :, pl.ds(k * group, group), :] = result.reshape(steps, requests, group, hdim)
        wide = result.astype(jnp.float32)
        square[0] += jnp.sum((wide * wide).reshape(groups, group, hdim), axis=1)
        return carry

    lax.fori_loop(0, kv, merge_head, 0)
    swap = send(square.at[0], square.at[1], square_sem.at[0], square_sem.at[1], {"tp": 1 - core})
    swap.start()
    swap.wait()
    mean = jnp.sum(square[0] + square[1], axis=-1, keepdims=True) / total_width
    scale = lax.rsqrt(mean + 1e-05)
    for t in range(steps):
        for g in range(requests):
            row = t * requests + g
            wide = attn[t, g].astype(jnp.float32)
            out[t, g] = (wide * scale[row : row + 1, :] * gain[...]).astype(out.dtype)

    for j in range(1, lines + 1):
        for i in range(1, plane):
            ship(j, i).wait_send()
        if j < lines:
            for copy in ask(j) + reply(j):
                copy.wait_send()


def attend(query, count, bias, gain, tiles, outgoing, cap, plane):
    steps, requests, heads, hdim = query.shape
    kv, page = tiles.shape[2:4]
    lines = outgoing.shape[0] // plane
    rows = steps * requests * heads // kv
    vmem = pl.BlockSpec(memory_space=pltpu.VMEM)
    dma = pltpu.SemaphoreType.DMA
    return pl.pallas_call(
        functools.partial(attend_kernel, cap, plane, lines, heads * hdim * lax.axis_size("tp")),
        out_shape=jax.ShapeDtypeStruct(query.shape, jnp.bfloat16),
        in_specs=[vmem] * 5 + [pl.BlockSpec(memory_space=pl.ANY)],
        out_specs=vmem,
        scratch_shapes=[
            pltpu.VMEM((lines, plane) + outgoing.shape[1:], jnp.bfloat16),
            pltpu.VMEM((lines,) + query.shape, jnp.bfloat16),
            pltpu.VMEM(count.shape, jnp.bfloat16),
            pltpu.VMEM((lines, kv, rows, hdim), jnp.bfloat16),
            pltpu.VMEM((lines, kv, 1, rows), jnp.float32),
            pltpu.VMEM((lines, kv, rows, hdim), jnp.bfloat16),
            pltpu.VMEM((lines, kv, 1, rows), jnp.float32),
            pltpu.VMEM((kv, rows, hdim), jnp.float32),
            pltpu.VMEM((kv, rows, 1), jnp.float32),
            pltpu.VMEM((kv, rows, 1), jnp.float32),
            pltpu.VMEM(query.shape, jnp.bfloat16),
            pltpu.VMEM((2, steps * requests, hdim), jnp.float32),
            dma((lines,)),
            dma((lines, plane)),
            dma((lines, plane)),
        ]
        + [dma((lines,))] * 8
        + [dma((2,))],
        compiler_params=pltpu.CompilerParams(
            vmem_limit_bytes=VMEM_LIMIT, collective_id=0, has_side_effects=True
        ),
        name="attend",
    )(query, count, bias, gain, tiles, outgoing)


def filled_tail(unfinished, fresh, fill):
    offset = jnp.arange(unfinished.shape[2], dtype=jnp.int32)[None, None, :, None, None]
    out = unfinished
    for s in range(fresh.shape[0]):
        out = jnp.where(offset == fill[:, None, None, None, None] + s, fresh[s][:, :, None], out)
    return out


def body(query, fresh, unfinished, store, table, history, fill, sender, target, switch, gain):
    replicas = lax.axis_size("rep")
    steps, requests, heads, hdim = query.shape
    cap = max(2, 2 * sender.shape[0] // replicas)
    plane = math.gcd(4, replicas)
    tiles = jnp.concatenate([store, filled_tail(unfinished, fresh, fill)], 0)
    tiles = jnp.transpose(tiles, (0, 1, 3, 2, 4))
    outgoing, count, bias = pack(
        tiles, sender, target, table, history, fill, switch, steps, replicas, cap, plane
    )
    normed = attend(query, count, bias, gain.reshape(heads, hdim), tiles, outgoing, cap, plane)
    return normed.reshape(steps, requests, heads * hdim)


def solution(mesh):
    placed = (
        P(None, "rep", "tp", None),
        P(None, "rep", None, "tp", None),
        P("rep", None, None, "tp", None),
        P("rep", None, None, "tp", None),
        P("rep", None),
        P("rep"),
        P("rep"),
        P("rep"),
        P("rep", None),
        P("rep"),
        P("tp"),
    )
    return jax.shard_map(
        body, mesh=mesh, in_specs=placed, out_specs=P(None, "rep", "tp"), check_vma=False
    )
```

time: 128 us -> 73.3 us (0.57)
  the two profiles are of different devices: /device:TPU:15 before, /device:TPU:0 now
where the time goes in v2:
time: 73.3 us; the launch traced here: 73 us
  Pallas kernels  65.3 us (89%)
  local copies, waits for them, and re-layouts  4.98 us (7%)
  other arithmetic  2.67 us (4%)
    pallas_call x1, Pallas kernels, attend(): pl.pallas_call(functools.partial(attend_kernel, cap, plane, lines, heads...  59.9 us
    pallas_call x1, Pallas kernels, pack(): pl.pallas_call(functools.partial(pack_kernel, cap, plane), out_shape=(jax...  5.32 us
    unnamed x16, local copies, waits for them, and re-layouts  3.46 us

profile of v2, /device:TPU:0, one launch (start us, length us, event | category | flops | bytes accessed | tf_op | source)
XLA Modules:
  0.0 73.0 jit_solution(13553363487405474263)
XLA Ops:
  0.0 0.7 broadcast_add_fusion.2
  0.7 0.7 iota_compare_fusion
  1.4 0.1 iota_compare_fusion.1
  1.5 0.7 %copy.14.target = s32[64,1]{1,0:T(8,128)S(1)} copy(s32[64,1]{0,1:T(1,128)} %param.19) | data formatting | bytes 512 | tf_op args[8]
  2.2 0.8 %slice_bitcast_fusion.3 = (bf16[4,2,4,128]{3,2,1,0:T(4,128)(2,1)S(1)}, bf16[4,2,4,128]{3,2,1,0:T(4,128)(2,1)S(1)}, bf16[4,2,4,128]{3,2,1,0:T(4,128)(2,1)S(1)}, bf16[4,2,4,128]{3,2,1,0:T(4,128)(2,1)S(1)}) fusion(bf16[4,4,2,4,128]{4,3,2,1,0:T(4,128)(2,1)} %param.12), kind=kLoop, calls=%fused_computation.8 | loop fusion | bytes 65536 | tf_op jit(solution)/shard_map/jit(_where)/broadcast_in_dim | solution.py:386
  3.0 1.0 %fusion.2 = bf16[4,2,16,4,128]{4,2,3,1,0:T(8,128)(2,1)S(1)} fusion(bf16[4,2,16,4,128]{4,3,2,1,0:T(4,128)(2,1)} %param.13, pred[4,16]{1,0:T(4,128)(4,1)S(1)} %get-tuple-element.20, pred[4,16]{1,0:T(4,128)(4,1)S(1)} %get-tuple-element.18, pred[4,16]{1,0:T(4,128)(4,1)S(1)} %get-tuple-element.19, pred[4,16]{1,0:T(4,128)(4,1)S(1)} %get-tuple-element.21, ...), kind=kLoop, calls=%fused_computation.4 | loop fusion | flops 262144 | bytes 295168 | tf_op jit(solution)/shard_map/jit(_where)/select_n | solution.py:386
  4.0 2.2 %copy.13 = bf16[64,2,16,4,128]{4,2,3,1,0:T(8,128)(2,1)S(1)} copy(bf16[64,2,16,4,128]{4,3,2,1,0:T(4,128)(2,1)} %param.14) | data formatting | bytes 4194304 | tf_op args[3]
  6.2 0.0 copy-start.2
  6.2 0.0 copy-start.3
  6.2 0.0 copy-start.4
  6.3 0.0 copy-start.5
  6.3 0.0 copy-start.6
  6.3 0.2 maximum_bitcast_fusion.tiles
  6.5 0.4 copy-done.2
  6.9 0.0 copy-done.3
  6.9 0.0 copy-done.4
  6.9 0.0 copy-done.5
  6.9 0.0 copy-done.6
  6.9 0.0 copy-start
  7.0 5.3 %pack.1 = (bf16[16,65,16,128]{3,2,1,0:T(8,128)(2,1)}, bf16[4,16,512]{2,1,0:T(8,128)(2,1)S(1)}, f32[16,1088]{1,0:T(8,128)S(1)}) custom-call(s32[64]{0:T(128)S(1)} %copy-done.4, s32[64,1]{1,0:T(8,128)S(1)} %copy.14.target, s32[4]{0:T(128)S(1)} %copy-done.5, s32[4]{0:T(128)S(1)} %copy-done.2, s32[4]{0:T(128)S(1)} %copy-done.6, ...), custom_call_target="tpu_custom_call" | custom-call | tf_op jit(solution)/shard_map/pack/pallas_call | solution.py:111
  12.3 0.0 copy-done
  12.3 0.0 copy-done.1
  12.3 59.9 %attend.1 = bf16[4,4,64,128]{3,2,1,0:T(8,128)(2,1)S(1)} custom-call(bf16[4,4,64,128]{3,2,1,0:T(8,128)(2,1)S(1)} %copy-done, bf16[4,16,512]{2,1,0:T(8,128)(2,1)S(1)} %get-tuple-element.8.count, f32[16,1088]{1,0:T(8,128)S(1)} %get-tuple-element.9.bias, f32[64,128]{1,0:T(8,128)S(1)} %bitcast.13, bf16[68,2,4,16,128]{4,3,2,1,0:T(8,128)(2,1)S(1)} %maximum_bitcast_fusion.tiles, ...), custom_call_target="tpu_custom_call" | custom-call | tf_op jit(solution)/shard_map/attend/pallas_call | solution.py:351
  72.2 0.8 %reshape.108 = bf16[4,4,8192]{2,1,0:T(4,128)(2,1)} reshape(bf16[4,4,64,128]{3,2,1,0:T(8,128)(2,1)S(1)} %attend.1) | data formatting | bytes 524288 | tf_op jit(solution)/shard_map/reshape | solution.py:401
  (1 shorter events, 0.0 us)
Async XLA Ops:
  6.2 0.7 copy-start.2
  6.2 0.7 copy-start.3
  6.2 0.7 copy-start.4
  6.3 0.7 copy-start.5
  6.3 0.7 copy-start.6
  6.9 5.3 %copy-start = (bf16[4,4,64,128]{3,2,1,0:T(8,128)(2,1)S(1)}, bf16[4,4,64,128]{3,2,1,0:T(8,128)(2,1)}, u32[]{:S(2)}) copy-start(bf16[4,4,64,128]{3,2,1,0:T(8,128)(2,1)} %query.1) | copy-start | bytes 786436
  6.9 5.3 %copy-start.1 = (f32[8192]{0:T(1024)S(1)}, f32[8192]{0:T(1024)}, u32[]{:S(2)}) copy-start(f32[8192]{0:T(1024)} %param.21) | copy-start | bytes 98308

commit v3 on v2

v3 whole, which is shorter than its diff:
```python
import functools
import math

import jax
import jax.numpy as jnp
from jax import lax
from jax.experimental import pallas as pl
from jax.experimental.pallas import tpu as pltpu
from jax.sharding import PartitionSpec as P

NEG = -1e30
LOG2E = 1.4426950408889634
VMEM_LIMIT = 50 * 1024 * 1024


def counts_of(table, history, first, pages, page):
    requests, entries = table.shape
    offset = lax.broadcasted_iota(jnp.int32, (page, entries), 0)
    position = lax.broadcasted_iota(jnp.int32, (page, entries), 1) * page + offset
    named = lax.broadcasted_iota(jnp.int32, (pages, entries), 0) + first
    per_page = []
    for g in range(requests):
        inside = jnp.where(position < history[g], 1.0, 0.0).astype(jnp.bfloat16)
        hit = jnp.where(table[g : g + 1, :] == named, 1.0, 0.0).astype(jnp.bfloat16)
        per_page.append(
            lax.dot_general(inside, hit, (((1,), (1,)), ((), ())), preferred_element_type=jnp.float32)
        )
    tokens = pages * page
    spread = (
        lax.broadcasted_iota(jnp.int32, (pages, tokens), 1) // page
        == lax.broadcasted_iota(jnp.int32, (pages, tokens), 0)
    )
    wide = jnp.dot(
        jnp.concatenate(per_page, 0).astype(jnp.bfloat16),
        jnp.where(spread, 1.0, 0.0).astype(jnp.bfloat16),
        preferred_element_type=jnp.float32,
    )
    own = (
        lax.broadcasted_iota(jnp.int32, (page, tokens), 1) % page
        == lax.broadcasted_iota(jnp.int32, (page, tokens), 0)
    )
    return [
        jnp.sum(jnp.where(own, wide[g * page : (g + 1) * page], 0.0), axis=0, keepdims=True)
        for g in range(requests)
    ]


def bias_of(count):
    return jnp.where(count > 0.0, jnp.log2(jnp.maximum(count, 1.0)), NEG)


def head_scores(query, keys, bias):
    rows, hdim = query.shape
    scores = lax.dot_general(query, keys, (((1,), (1,)), ((), ())), preferred_element_type=jnp.float32)
    groups = bias.shape[0]
    scores = scores.reshape(groups, rows // groups, -1) * (LOG2E / math.sqrt(hdim)) + bias[:, None, :]
    return scores.reshape(rows, -1)


def plan_kernel(cap, pool, sender, target, fill, switch, unfinished, fresh, source, length, tails, held):
    requests, parts, kv, page, hdim = unfinished.shape
    slots = source.shape[0]
    for s in range(slots):
        source[s] = 0
        length[s] = 0
    for d in range(slots // cap):
        held[d] = d * cap

    def place(e, carry):
        d = target[e]
        slot = held[d]
        held[d] = slot + 1
        tile = sender[e]
        owner = jnp.maximum(tile - pool, 0)
        source[slot] = tile
        length[slot] = jnp.where(tile >= pool, fill[owner] + switch[owner], page)
        return carry

    lax.fori_loop(0, target.shape[0], place, 0)
    offset = lax.broadcasted_iota(jnp.int32, (page, hdim), 0)
    for g in range(requests):
        for c in range(parts):
            steps = [fresh[s, g, c].astype(jnp.float32) for s in range(fresh.shape[0])]
            for k in range(kv):
                block = unfinished[g, c, k].astype(jnp.float32)
                for s in range(len(steps)):
                    block = jnp.where(offset == fill[g] + s, steps[s][k : k + 1, :], block)
                tails[g, c, k] = block.astype(tails.dtype)


def plan(sender, target, fill, switch, unfinished, fresh, pool, replicas, cap):
    smem = pl.BlockSpec(memory_space=pltpu.SMEM)
    vmem = pl.BlockSpec(memory_space=pltpu.VMEM)
    slots = jax.ShapeDtypeStruct((replicas * cap,), jnp.int32)
    return pl.pallas_call(
        functools.partial(plan_kernel, cap, pool),
        out_shape=(slots, slots, jax.ShapeDtypeStruct(unfinished.shape, unfinished.dtype)),
        in_specs=[smem] * 4 + [vmem] * 2,
        out_specs=(smem, smem, vmem),
        scratch_shapes=[pltpu.SMEM((replicas,), jnp.int32)],
        compiler_params=pltpu.CompilerParams(vmem_limit_bytes=VMEM_LIMIT),
        name="plan",
    )(sender, target, fill, switch, unfinished, fresh)


def partial(query, keys, values, bias):
    scores = head_scores(query, keys, bias)
    best = jnp.max(scores, axis=-1, keepdims=True)
    probs = jnp.exp2(scores - best)
    total = jnp.sum(probs, axis=-1, keepdims=True)
    return jnp.dot(probs.astype(jnp.bfloat16), values, preferred_element_type=jnp.float32), best, total


def diagonal(size):
    return lax.broadcasted_iota(jnp.int32, (size, size), 0) == lax.broadcasted_iota(jnp.int32, (size, size), 1)


def attend_kernel(
    cap, plane, lines, total_width,
    source, length, history, fill, switch,
    query, table, gain, tiles, tails,
    out,
    outgoing, count, bias, last_bias, arrived, asked, asked_count, answer, answer_log, given, given_log, mixed, top, total, attn, square,
    tile_send, tile_recv, ask_send, ask_recv, count_send, count_recv,
    answer_send, answer_recv, log_send, log_recv, square_sem,
):
    steps, requests, heads, hdim = query.shape
    pool, parts, kv, page, _ = tiles.shape
    group = heads // kv
    groups = steps * requests
    rows = groups * group
    tokens = plane * cap * page
    me = lax.axis_index("rep")
    core = lax.axis_index("tp")
    line, place = lax.div(me, plane), lax.rem(me, plane)

    def peer(a_line, a_place):
        return {"rep": a_line * plane + a_place}

    def send(source, target, send_sem, recv_sem, device):
        return pltpu.make_async_remote_copy(
            src_ref=source, dst_ref=target, send_sem=send_sem, recv_sem=recv_sem,
            device_id=device, device_id_type=pl.DeviceIdType.MESH,
        )

    def line_at(step):
        return lax.rem(line + step, lines)

    def line_back(step):
        return lax.rem(line + lines - step, lines)

    def place_at(step):
        if plane == 4:
            y, x = lax.div(place, 2), lax.rem(place, 2)
            return lax.rem(y + step // 2, 2) * 2 + lax.rem(x + step % 2, 2)
        return lax.rem(place + step, plane)

    barrier = pltpu.get_barrier_semaphore()
    for j in range(1, lines):
        pl.semaphore_signal(barrier, inc=1, device_id=peer(line_at(j), place), device_id_type=pl.DeviceIdType.MESH)
    for i in range(1, plane):
        pl.semaphore_signal(barrier, inc=1, device_id=peer(line, place_at(i)), device_id_type=pl.DeviceIdType.MESH)
    pl.semaphore_signal(barrier, inc=1, device_id={"tp": 1 - core}, device_id_type=pl.DeviceIdType.MESH)
    pl.semaphore_wait(barrier, lines + plane - 1)

    def ask(j):
        to = line_at(j)
        return send(query, asked.at[line], ask_send.at[to], ask_recv.at[line], peer(to, place))

    def ask_counts(j):
        to = line_at(j)
        return send(
            count.at[to], asked_count.at[line], count_send.at[to], count_recv.at[line], peer(to, place)
        )

    def ship(j, i):
        to = line_at(j)
        mate = place_at(i)
        return send(
            outgoing.at[to * plane + mate], arrived.at[to, place],
            tile_send.at[to, mate], tile_recv.at[to, place], peer(line, mate),
        )

    def reply(j):
        to = line_at(j)
        return (
            send(answer.at[to], given.at[line], answer_send.at[to], answer_recv.at[line], peer(to, place)),
            send(answer_log.at[to], given_log.at[line], log_send.at[to], log_recv.at[line], peer(to, place)),
        )

    lane = lax.broadcasted_iota(jnp.int32, (page, hdim), 1)

    def fill_block(block, receiver):
        def one_slot(rank, mask):
            tile = source[receiver * cap + rank]
            for c in range(parts):
                for k in range(kv):
                    block[(c * kv + k) * cap + rank] = jnp.where(
                        tile >= pool,
                        tails[jnp.maximum(tile - pool, 0), c, k],
                        tiles[jnp.minimum(tile, pool - 1), c, k],
                    )
            lo = rank * page
            return jnp.where((lane >= lo) & (lane < lo + length[receiver * cap + rank]), 1.0, mask)

        mask = lax.fori_loop(0, cap, one_slot, jnp.zeros((page, hdim), jnp.float32))
        block[parts * kv * cap] = mask.astype(jnp.bfloat16)

    order = list(range(plane - 1, 0, -1))
    for j in range(1, lines + 1):
        to = line_at(j)
        for i in order:
            receiver = to * plane + place_at(i)
            fill_block(outgoing.at[receiver], receiver)
            ship(j, i).start()
        if j < lines:
            ask(lines - j).start()
    for j in range(1, lines + 1):
        fill_block(arrived.at[line_at(j), place], line_at(j) * plane + place)

    tokens_in = counts_of(table, history, pool, lines * plane * cap, page)
    for to in range(lines):
        parts_of = [
            jnp.where(t >= switch[g], tokens_in[g][:, to * tokens : (to + 1) * tokens], 0.0)
            for t in range(steps)
            for g in range(requests)
        ]
        count[to] = jnp.concatenate(parts_of, 0).astype(count.dtype)
    for j in range(1, lines):
        ask_counts(lines - j).start()

    own = counts_of(table, history, 0, pool, page)
    tail = lax.broadcasted_iota(jnp.int32, (1, requests * page), 1)
    for t in range(steps):
        for g in range(requests):
            row = t * requests + g
            bias[row : row + 1, : pool * page] = bias_of(own[g])
            seen = (tail // page == g) & (tail % page < fill[g] + t + 1)
            bias[row : row + 1, pool * page :] = jnp.where(seen, 0.0, NEG)

    def pool_head(k, carry):
        q = query[:, :, pl.ds(k * group, group), :].reshape(rows, hdim)
        both = [
            jnp.concatenate(
                [tiles[:, c, k].reshape(pool * page, hdim), tails[:, c, k].reshape(requests * page, hdim)], 0
            )
            for c in range(2)
        ]
        mixed[k], top[k], total[k] = partial(q, both[0], both[1], bias[...])
        return carry

    lax.fori_loop(0, kv, pool_head, 0)

    width = cap * page
    repeat = (
        lax.broadcasted_iota(jnp.int32, (hdim, tokens), 1) % width
        == lax.broadcasted_iota(jnp.int32, (hdim, tokens), 0)
    )
    repeat = jnp.where(repeat, 1.0, 0.0).astype(jnp.bfloat16)
    mine = (
        lax.broadcasted_iota(jnp.int32, (plane, tokens), 1) // width
        == lax.broadcasted_iota(jnp.int32, (plane, tokens), 0)
    )
    eye = diagonal(rows)

    def ship_in(to, mate):
        return send(
            outgoing.at[to * plane + mate], arrived.at[to, mate], tile_send.at[to, mate], tile_recv.at[to, mate],
            peer(line, mate),
        )

    def filled(to):
        here = arrived[to, :, 2 * kv * cap, 0, :]
        spread = jnp.dot(here, repeat, preferred_element_type=jnp.float32)
        return jnp.sum(jnp.where(mine, spread, 0.0), axis=0, keepdims=True)

    def arrivals(to, k):
        keys = arrived[to, :, pl.ds(k * cap, cap)].reshape(tokens, hdim)
        values = arrived[to, :, pl.ds((kv + k) * cap, cap)].reshape(tokens, hdim)
        return keys, values

    for j in range(1, lines):
        to = line_at(j)
        for i in order:
            mate = place_at(i)
            ship_in(to, mate).wait_recv()
        send(query, asked.at[to], ask_send.at[to], ask_recv.at[to], peer(to, place)).wait_recv()
        send(
            count.at[to], asked_count.at[to], count_send.at[to], count_recv.at[to], peer(to, place)
        ).wait_recv()
        set_bias = bias_of(asked_count[to].astype(jnp.float32) * filled(to))

        def set_head(k, carry):
            q = asked[to, :, :, pl.ds(k * group, group), :].reshape(rows, hdim)
            keys, values = arrivals(to, k)
            part, best, amount = partial(q, keys, values, set_bias)
            answer[to, k] = (part / amount).astype(jnp.bfloat16)
            log = best + jnp.log2(amount)
            answer_log[to, k] = jnp.sum(jnp.where(eye, log, 0.0), axis=0, keepdims=True)
            return carry

        lax.fori_loop(0, kv, set_head, 0)
        for copy in reply(j):
            copy.start()

    for j in range(1, lines):
        to = line_at(j)
        send(answer.at[to], given.at[to], answer_send.at[to], answer_recv.at[to], peer(to, place)).wait_recv()
        send(answer_log.at[to], given_log.at[to], log_send.at[to], log_recv.at[to], peer(to, place)).wait_recv()

    def merge_head(k, carry):
        logs = []
        high = top[k]
        for j in range(1, lines):
            log = jnp.sum(jnp.where(eye, given_log[line_at(j), k], 0.0), axis=1, keepdims=True)
            logs.append(log)
            high = jnp.maximum(high, log)
        old = jnp.exp2(top[k] - high)
        whole = mixed[k] * old
        amount = total[k] * old
        for j in range(1, lines):
            share = jnp.exp2(logs[j - 1] - high)
            whole = whole + given[line_at(j), k].astype(jnp.float32) * share
            amount = amount + share
        mixed[k], total[k], top[k] = whole, amount, high
        return carry

    lax.fori_loop(0, kv, merge_head, 0)
    square[0] = jnp.zeros_like(square[0])

    for i in [0] + order:
        mate = place_at(i)
        if i > 0:
            ship_in(line, mate).wait_recv()
        here = arrived[line, mate, parts * kv * cap, 0:1, :].astype(jnp.float32)
        for m in range(plane):
            part = count[line, :, m * width : (m + 1) * width].astype(jnp.float32)
            mine_count = part if m == 0 else jnp.where(mate == m, part, mine_count)
        last_bias[...] = bias_of(mine_count * here[:, :width])

        def last_head(k, carry, mate=mate, last=i == order[-1]):
            q = query[:, :, pl.ds(k * group, group), :].reshape(rows, hdim)
            keys = arrived[line, mate, pl.ds(k * cap, cap)].reshape(width, hdim)
            values = arrived[line, mate, pl.ds((kv + k) * cap, cap)].reshape(width, hdim)
            part, best, amount = partial(q, keys, values, last_bias[...])
            high = jnp.maximum(best, top[k])
            fresh, old = jnp.exp2(best - high), jnp.exp2(top[k] - high)
            whole = part * fresh + mixed[k] * old
            amount = amount * fresh + total[k] * old
            if not last:
                mixed[k], total[k], top[k] = whole, amount, high
                return carry
            result = (whole / amount).astype(jnp.bfloat16)
            attn[:, :, pl.ds(k * group, group), :] = result.reshape(steps, requests, group, hdim)
            wide = result.astype(jnp.float32)
            square[0] += jnp.sum((wide * wide).reshape(groups, group, hdim), axis=1)
            return carry

        lax.fori_loop(0, kv, last_head, 0)

    swap = send(square.at[0], square.at[1], square_sem.at[0], square_sem.at[1], {"tp": 1 - core})
    swap.start()
    swap.wait()
    mean = jnp.sum(square[0] + square[1], axis=-1, keepdims=True) / total_width
    scale = lax.rsqrt(mean + 1e-05)
    for t in range(steps):
        for g in range(requests):
            row = t * requests + g
            wide = attn[t, g].astype(jnp.float32)
            out[t, g] = (wide * scale[row : row + 1, :] * gain[...]).astype(out.dtype)

    for j in range(1, lines + 1):
        for i in range(1, plane):
            ship(j, i).wait_send()
        if j < lines:
            for copy in (ask(j), ask_counts(j)) + reply(j):
                copy.wait_send()


def attend(source, length, history, fill, switch, query, table, gain, tiles, tails, cap, plane, lines):
    steps, requests, heads, hdim = query.shape
    pool, parts, kv, page, _ = tiles.shape
    rows = steps * requests * heads // kv
    width = cap * page
    smem = pl.BlockSpec(memory_space=pltpu.SMEM)
    vmem = pl.BlockSpec(memory_space=pltpu.VMEM)
    dma = pltpu.SemaphoreType.DMA
    block = (parts * kv * cap + 1, page, hdim)
    return pl.pallas_call(
        functools.partial(attend_kernel, cap, plane, lines, heads * hdim * lax.axis_size("tp")),
        out_shape=jax.ShapeDtypeStruct(query.shape, jnp.bfloat16),
        in_specs=[smem] * 5 + [vmem] * 5,
        out_specs=vmem,
        scratch_shapes=[
            pltpu.VMEM((lines * plane,) + block, jnp.bfloat16),
            pltpu.VMEM((lines, steps * requests, plane * width), jnp.bfloat16),
            pltpu.VMEM((steps * requests, (pool + requests) * page), jnp.float32),
            pltpu.VMEM((steps * requests, width), jnp.float32),
            pltpu.VMEM((lines, plane) + block, jnp.bfloat16),
            pltpu.VMEM((lines,) + query.shape, jnp.bfloat16),
            pltpu.VMEM((lines, steps * requests, plane * width), jnp.bfloat16),
            pltpu.VMEM((lines, kv, rows, hdim), jnp.bfloat16),
            pltpu.VMEM((lines, kv, 1, rows), jnp.float32),
            pltpu.VMEM((lines, kv, rows, hdim), jnp.bfloat16),
            pltpu.VMEM((lines, kv, 1, rows), jnp.float32),
            pltpu.VMEM((kv, rows, hdim), jnp.float32),
            pltpu.VMEM((kv, rows, 1), jnp.float32),
            pltpu.VMEM((kv, rows, 1), jnp.float32),
            pltpu.VMEM(query.shape, jnp.bfloat16),
            pltpu.VMEM((2, steps * requests, hdim), jnp.float32),
            dma((lines, plane)),
            dma((lines, plane)),
        ]
        + [dma((lines,))] * 8
        + [dma((2,))],
        compiler_params=pltpu.CompilerParams(
            vmem_limit_bytes=VMEM_LIMIT, collective_id=0, has_side_effects=True
        ),
        name="attend",
    )(source, length, history, fill, switch, query, table, gain, tiles, tails)


def body(query, fresh, unfinished, store, table, history, fill, sender, target, switch, gain):
    replicas = lax.axis_size("rep")
    steps, requests, heads, hdim = query.shape
    cap = max(2, 2 * sender.shape[0] // replicas)
    plane = math.gcd(4, replicas)
    tiles = jnp.transpose(store, (0, 1, 3, 2, 4))
    source, length, tails = plan(
        sender, target.reshape(-1), fill, switch, jnp.transpose(unfinished, (0, 1, 3, 2, 4)), fresh,
        store.shape[0], replicas, cap,
    )
    normed = attend(
        source, length, history, fill, switch, query, table, gain.reshape(heads, hdim), tiles, tails,
        cap, plane, replicas // plane,
    )
    return normed.reshape(steps, requests, heads * hdim)


def solution(mesh):
    placed = (
        P(None, "rep", "tp", None),
        P(None, "rep", None, "tp", None),
        P("rep", None, None, "tp", None),
        P("rep", None, None, "tp", None),
        P("rep", None),
        P("rep"),
        P("rep"),
        P("rep"),
        P("rep", None),
        P("rep"),
        P("tp"),
    )
    return jax.shard_map(
        body, mesh=mesh, in_specs=placed, out_specs=P(None, "rep", "tp"), check_vma=False
    )
```

time: 73.3 us -> 92.6 us (1.26)
  the two profiles are of different devices: /device:TPU:0 before, /device:TPU:25 now
where the time goes in v3:
time: 92.6 us; the launch traced here: 92.3 us
  Pallas kernels  84.8 us (92%)
  local copies, waits for them, and re-layouts  7.41 us (8%)
    pallas_call x1, Pallas kernels, attend(): pl.pallas_call(functools.partial(attend_kernel, cap, plane, lines, heads...  82.6 us
    unnamed x24, local copies, waits for them, and re-layouts  6.64 us
    pallas_call x1, Pallas kernels, plan(): pl.pallas_call(functools.partial(plan_kernel, cap, pool), out_shape=(slot...  2.15 us

profile of v3, /device:TPU:25, one launch (start us, length us, event | category | flops | bytes accessed | tf_op | source)
XLA Modules:
  0.0 92.3 jit_solution(551554251192744173)
XLA Ops:
  0.0 0.9 copy.17
  0.9 0.0 copy-start.2
  0.9 0.7 copy-done.2
  1.7 0.0 copy-start.4
  1.7 0.7 copy-done.4
  2.3 0.7 copy-done.6
  3.0 0.7 copy-done.9
  3.7 0.7 copy-done.10
  4.3 2.1 %plan.1 = (s32[128]{0:T(128)S(1)}, s32[128]{0:T(128)S(1)}, bf16[4,2,4,16,128]{4,3,2,1,0:T(8,128)(2,1)S(1)}) custom-call(s32[64]{0:T(128)S(1)} %copy-done.9, s32[64]{0:T(128)S(1)} %bitcast.13, s32[4]{0:T(128)S(1)} %copy-done.4, s32[4]{0:T(128)S(1)} %copy-done.6, bf16[4,2,4,16,128]{4,3,2,1,0:T(8,128)(2,1)S(1)} %bitcast.11, bf16[4,4,2,4,128]{4,3,2,1,0:T(4,128)(2,1)S(1)} %copy-done.2), custom_call_target="tpu_custom_call" | custom-call | tf_op jit(solution)/shard_map/plan/pallas_call | solution.py:95
  6.5 0.0 copy-start
  6.5 0.0 copy-start.1
  6.5 0.0 copy-start.3
  6.5 0.0 copy-start.5
  6.5 0.0 copy-start.7
  6.5 0.0 copy-start.8
  6.5 2.3 %copy.16 = bf16[64,2,16,4,128]{4,2,3,1,0:T(8,128)(2,1)S(1)} copy(bf16[64,2,16,4,128]{4,3,2,1,0:T(4,128)(2,1)} %param.14) | data formatting | bytes 4194304 | tf_op args[3]
  8.9 0.0 copy-done
  8.9 0.0 copy-done.1
  8.9 0.0 copy-done.3
  8.9 0.0 copy-done.5
  8.9 0.0 copy-done.7
  8.9 0.0 copy-done.8
  8.9 82.6 %attend.1 = bf16[4,4,64,128]{3,2,1,0:T(8,128)(2,1)S(1)} custom-call(s32[128]{0:T(128)S(1)} %get-tuple-element.8.source, s32[128]{0:T(128)S(1)} %get-tuple-element.9.length, s32[4]{0:T(128)S(1)} %copy-done.8, s32[4]{0:T(128)S(1)} %copy-done.5, s32[4]{0:T(128)S(1)} %copy-done.7, bf16[4,4,64,128]{3,2,1,0:T(8,128)(2,1)S(1)} %copy-done, s32[4,128]{1,0:T(4,128)S(1)} %copy-done.3, ...), custom_call_target="tpu_custom_call" | custom-call | tf_op jit(solution)/shard_map/attend/pallas_call | solution.py:389
  91.6 0.8 reshape.11
  (3 shorter events, 0.0 us)
Async XLA Ops:
  0.9 0.8 copy-start.2
  1.7 0.7 copy-start.4
  2.3 0.7 copy-start.6
  3.0 0.7 copy-start.9
  3.7 0.7 copy-start.10
  6.5 2.4 %copy-start = (bf16[4,4,64,128]{3,2,1,0:T(8,128)(2,1)S(1)}, bf16[4,4,64,128]{3,2,1,0:T(8,128)(2,1)}, u32[]{:S(2)}) copy-start(bf16[4,4,64,128]{3,2,1,0:T(8,128)(2,1)} %query.1) | copy-start | bytes 786436
  6.5 2.4 %copy-start.1 = (f32[8192]{0:T(1024)S(1)}, f32[8192]{0:T(1024)}, u32[]{:S(2)}) copy-start(f32[8192]{0:T(1024)} %param.21) | copy-start | bytes 98308
  6.5 2.4 %copy-start.3 = (s32[4,128]{1,0:T(4,128)S(1)}, s32[4,128]{1,0:T(4,128)}, u32[]{:S(2)}) copy-start(s32[4,128]{1,0:T(4,128)} %table.1) | copy-start | bytes 6148
  6.5 2.4 %copy-start.5 = (s32[4]{0:T(128)S(1)}, s32[4]{0:T(128)}, u32[]{:S(2)}) copy-start(s32[4]{0:T(128)} %fill.3) | copy-start | bytes 52
  6.5 2.4 %copy-start.7 = (s32[4]{0:T(128)S(1)}, s32[4]{0:T(128)}, u32[]{:S(2)}) copy-start(s32[4]{0:T(128)} %switch.3) | copy-start | bytes 52
  6.5 2.4 %copy-start.8 = (s32[4]{0:T(128)S(1)}, s32[4]{0:T(128)}, u32[]{:S(2)}) copy-start(s32[4]{0:T(128)} %history.1) | copy-start | bytes 52

commit v4 on v3

--- a/solution.py
+++ b/solution.py
@@ -57,9 +57,10 @@
     return scores.reshape(rows, -1)
 
 
-def plan_kernel(cap, pool, sender, target, fill, switch, unfinished, fresh, source, length, tails, held):
+def plan_kernel(cap, sender, target, fill, switch, unfinished, fresh, tiles, source, length, tails, held):
     requests, parts, kv, page, hdim = unfinished.shape
     slots = source.shape[0]
+    pool = tiles.shape[0]
     for s in range(slots):
         source[s] = 0
         length[s] = 0
@@ -88,19 +89,19 @@
                 tails[g, c, k] = block.astype(tails.dtype)
 
 
-def plan(sender, target, fill, switch, unfinished, fresh, pool, replicas, cap):
+def plan(sender, target, fill, switch, unfinished, fresh, tiles, replicas, cap):
     smem = pl.BlockSpec(memory_space=pltpu.SMEM)
     vmem = pl.BlockSpec(memory_space=pltpu.VMEM)
     slots = jax.ShapeDtypeStruct((replicas * cap,), jnp.int32)
     return pl.pallas_call(
-        functools.partial(plan_kernel, cap, pool),
+        functools.partial(plan_kernel, cap),
         out_shape=(slots, slots, jax.ShapeDtypeStruct(unfinished.shape, unfinished.dtype)),
-        in_specs=[smem] * 4 + [vmem] * 2,
+        in_specs=[smem] * 4 + [vmem] * 2 + [pl.BlockSpec(memory_space=pl.ANY)],
         out_specs=(smem, smem, vmem),
         scratch_shapes=[pltpu.SMEM((replicas,), jnp.int32)],
         compiler_params=pltpu.CompilerParams(vmem_limit_bytes=VMEM_LIMIT),
         name="plan",
-    )(sender, target, fill, switch, unfinished, fresh)
+    )(sender, target, fill, switch, unfinished, fresh, tiles)
 
 
 def partial(query, keys, values, bias):
@@ -151,6 +152,8 @@
 
     def place_at(step):
         if plane == 4:
+            if step in (1, 2):
+                step = step + core * (3 - 2 * step)
             y, x = lax.div(place, 2), lax.rem(place, 2)
             return lax.rem(y + step // 2, 2) * 2 + lax.rem(x + step % 2, 2)
         return lax.rem(place + step, plane)
@@ -206,7 +209,7 @@
         mask = lax.fori_loop(0, cap, one_slot, jnp.zeros((page, hdim), jnp.float32))
         block[parts * kv * cap] = mask.astype(jnp.bfloat16)
 
-    order = list(range(plane - 1, 0, -1))
+    order = list(range(1, plane))
     for j in range(1, lines + 1):
         to = line_at(j)
         for i in order:
@@ -428,7 +431,7 @@
     tiles = jnp.transpose(store, (0, 1, 3, 2, 4))
     source, length, tails = plan(
         sender, target.reshape(-1), fill, switch, jnp.transpose(unfinished, (0, 1, 3, 2, 4)), fresh,
-        store.shape[0], replicas, cap,
+        tiles, replicas, cap,
     )
     normed = attend(
         source, length, history, fill, switch, query, table, gain.reshape(heads, hdim), tiles, tails,

time: 92.6 us -> 89.1 us (0.962)
  local copies, waits for them, and re-layouts: 7.41 us -> 3.99 us
    unnamed x24 -> x20, local copies, waits for them, and re-layouts: 6.64 us -> 3.22 us
where the time goes in v4:
time: 89.1 us; the launch traced here: 88.9 us
  Pallas kernels  84.8 us (95%)
  local copies, waits for them, and re-layouts  3.99 us (4%)
    pallas_call x1, Pallas kernels, attend(): pl.pallas_call(functools.partial(attend_kernel, cap, plane, lines, heads...  82.6 us
    unnamed x20, local copies, waits for them, and re-layouts  3.22 us
    pallas_call x1, Pallas kernels, plan(): pl.pallas_call(functools.partial(plan_kernel, cap), out_shape=(slots, slo...  2.15 us

profile of v4, /device:TPU:25, one launch (start us, length us, event | category | flops | bytes accessed | tf_op | source)
XLA Modules:
  0.0 88.9 jit_solution(14551423195123858677)
XLA Ops:
  0.0 0.9 %copy.17 = bf16[4,2,16,4,128]{4,2,3,1,0:T(8,128)(2,1)S(1)} copy(bf16[4,2,16,4,128]{4,3,2,1,0:T(4,128)(2,1)} %param.13) | data formatting | bytes 262144 | tf_op args[2]
  0.9 0.0 copy-start.1
  0.9 0.0 copy-start.4
  1.0 0.0 copy-start.5
  1.0 0.0 copy-start.6
  1.0 0.0 copy-start.7
  1.0 2.2 %copy.16 = bf16[64,2,16,4,128]{4,2,3,1,0:T(8,128)(2,1)S(1)} copy(bf16[64,2,16,4,128]{4,3,2,1,0:T(4,128)(2,1)} %param.14) | data formatting | bytes 4194304 | tf_op args[3]
  3.2 0.0 copy-start
  3.3 0.0 copy-start.2
  3.3 0.0 copy-start.3
  3.3 0.0 copy-start.8
  3.3 0.0 copy-done.1
  3.3 0.0 copy-done.4
  3.3 0.0 copy-done.5
  3.3 0.0 copy-done.6
  3.3 0.0 copy-done.7
  3.3 2.1 %plan.1 = (s32[128]{0:T(128)S(1)}, s32[128]{0:T(128)S(1)}, bf16[4,2,4,16,128]{4,3,2,1,0:T(8,128)(2,1)S(1)}) custom-call(s32[64]{0:T(128)S(1)} %copy-done.6, s32[64]{0:T(128)S(1)} %bitcast.14, s32[4]{0:T(128)S(1)} %copy-done.4, s32[4]{0:T(128)S(1)} %copy-done.5, bf16[4,2,4,16,128]{4,3,2,1,0:T(8,128)(2,1)S(1)} %bitcast.12, ...), custom_call_target="tpu_custom_call" | custom-call | tf_op jit(solution)/shard_map/plan/pallas_call | solution.py:96
  5.5 0.0 copy-done
  5.5 0.0 copy-done.2
  5.5 0.0 copy-done.3
  5.5 0.0 copy-done.8
  5.5 82.6 %attend.1 = bf16[4,4,64,128]{3,2,1,0:T(8,128)(2,1)S(1)} custom-call(s32[128]{0:T(128)S(1)} %get-tuple-element.8.source, s32[128]{0:T(128)S(1)} %get-tuple-element.9.length, s32[4]{0:T(128)S(1)} %copy-done.8, s32[4]{0:T(128)S(1)} %copy-done.4, s32[4]{0:T(128)S(1)} %copy-done.5, bf16[4,4,64,128]{3,2,1,0:T(8,128)(2,1)S(1)} %copy-done, s32[4,128]{1,0:T(4,128)S(1)} %copy-done.3, ...), custom_call_target="tpu_custom_call" | custom-call | tf_op jit(solution)/shard_map/attend/pallas_call | solution.py:392
  88.2 0.8 reshape.11
Async XLA Ops:
  0.9 2.4 %copy-start.1 = (bf16[4,4,2,4,128]{4,3,2,1,0:T(4,128)(2,1)S(1)}, bf16[4,4,2,4,128]{4,3,2,1,0:T(4,128)(2,1)}, u32[]{:S(2)}) copy-start(bf16[4,4,2,4,128]{4,3,2,1,0:T(4,128)(2,1)} %fresh.1) | copy-start | bytes 98308
  0.9 2.4 %copy-start.4 = (s32[4]{0:T(128)S(1)}, s32[4]{0:T(128)}, u32[]{:S(2)}) copy-start(s32[4]{0:T(128)} %fill.3) | copy-start | bytes 52
  1.0 2.4 %copy-start.5 = (s32[4]{0:T(128)S(1)}, s32[4]{0:T(128)}, u32[]{:S(2)}) copy-start(s32[4]{0:T(128)} %switch.3) | copy-start | bytes 52
  1.0 2.4 %copy-start.6 = (s32[64]{0:T(128)S(1)}, s32[64]{0:T(128)}, u32[]{:S(2)}) copy-start(s32[64]{0:T(128)} %sender.1) | copy-start | bytes 772
  1.0 2.4 %copy-start.7 = (s32[64,1]{0,1:T(1,128)S(1)}, s32[64,1]{0,1:T(1,128)}, u32[]{:S(2)}) copy-start(s32[64,1]{0,1:T(1,128)} %param.19) | copy-start | bytes 772
  3.2 2.3 %copy-start = (bf16[4,4,64,128]{3,2,1,0:T(8,128)(2,1)S(1)}, bf16[4,4,64,128]{3,2,1,0:T(8,128)(2,1)}, u32[]{:S(2)}) copy-start(bf16[4,4,64,128]{3,2,1,0:T(8,128)(2,1)} %query.1) | copy-start | bytes 786436
  3.3 2.3 %copy-start.2 = (f32[8192]{0:T(1024)S(1)}, f32[8192]{0:T(1024)}, u32[]{:S(2)}) copy-start(f32[8192]{0:T(1024)} %param.21) | copy-start | bytes 98308
  3.3 2.3 %copy-start.3 = (s32[4,128]{1,0:T(4,128)S(1)}, s32[4,128]{1,0:T(4,128)}, u32[]{:S(2)}) copy-start(s32[4,128]{1,0:T(4,128)} %table.1) | copy-start | bytes 6148
  3.3 2.3 %copy-start.8 = (s32[4]{0:T(128)S(1)}, s32[4]{0:T(128)}, u32[]{:S(2)}) copy-start(s32[4]{0:T(128)} %history.1) | copy-start | bytes 52

commit v5 on v4

--- a/solution.py
+++ b/solution.py
@@ -210,17 +210,14 @@
         block[parts * kv * cap] = mask.astype(jnp.bfloat16)
 
     order = list(range(1, plane))
-    for j in range(1, lines + 1):
-        to = line_at(j)
-        for i in order:
-            receiver = to * plane + place_at(i)
+
+    def launch(j, pieces):
+        for i in pieces:
+            receiver = line_at(j) * plane + place_at(i)
             fill_block(outgoing.at[receiver], receiver)
             ship(j, i).start()
-        if j < lines:
-            ask(lines - j).start()
-    for j in range(1, lines + 1):
-        fill_block(arrived.at[line_at(j), place], line_at(j) * plane + place)
-
+
+    launch(1, order[:1])
     tokens_in = counts_of(table, history, pool, lines * plane * cap, page)
     for to in range(lines):
         parts_of = [
@@ -229,8 +226,17 @@
             for g in range(requests)
         ]
         count[to] = jnp.concatenate(parts_of, 0).astype(count.dtype)
-    for j in range(1, lines):
+    if lines > 1:
+        ask(lines - 1).start()
+        ask_counts(lines - 1).start()
+    launch(1, order[1:])
+    for j in range(2, lines):
+        ask(lines - j).start()
         ask_counts(lines - j).start()
+    if lines > 1:
+        launch(2, order[:1])
+    for j in range(1, lines + 1):
+        fill_block(arrived.at[line_at(j), place], line_at(j) * plane + place)
 
     own = counts_of(table, history, 0, pool, page)
     tail = lax.broadcasted_iota(jnp.int32, (1, requests * page), 1)
@@ -305,11 +311,9 @@
         lax.fori_loop(0, kv, set_head, 0)
         for copy in reply(j):
             copy.start()
-
-    for j in range(1, lines):
-        to = line_at(j)
-        send(answer.at[to], given.at[to], answer_send.at[to], answer_recv.at[to], peer(to, place)).wait_recv()
-        send(answer_log.at[to], given_log.at[to], log_send.at[to], log_recv.at[to], peer(to, place)).wait_recv()
+        launch(j + 1, order[1:])
+        if j + 2 <= lines:
+            launch(j + 2, order[:1])
 
     def merge_head(k, carry):
         logs = []
@@ -328,10 +332,9 @@
         mixed[k], total[k], top[k] = whole, amount, high
         return carry
 
-    lax.fori_loop(0, kv, merge_head, 0)
     square[0] = jnp.zeros_like(square[0])
 
-    for i in [0] + order:
+    def last_source(i):
         mate = place_at(i)
         if i > 0:
             ship_in(line, mate).wait_recv()
@@ -341,7 +344,7 @@
             mine_count = part if m == 0 else jnp.where(mate == m, part, mine_count)
         last_bias[...] = bias_of(mine_count * here[:, :width])
 
-        def last_head(k, carry, mate=mate, last=i == order[-1]):
+        def last_head(k, carry, mate=mate, last=i == (order[-1] if order else 0)):
             q = query[:, :, pl.ds(k * group, group), :].reshape(rows, hdim)
             keys = arrived[line, mate, pl.ds(k * cap, cap)].reshape(width, hdim)
             values = arrived[line, mate, pl.ds((kv + k) * cap, cap)].reshape(width, hdim)
@@ -360,6 +363,16 @@
             return carry
 
         lax.fori_loop(0, kv, last_head, 0)
+
+    for i in [0] + order[:1]:
+        last_source(i)
+    for j in range(1, lines):
+        to = line_at(j)
+        send(answer.at[to], given.at[to], answer_send.at[to], answer_recv.at[to], peer(to, place)).wait_recv()
+        send(answer_log.at[to], given_log.at[to], log_send.at[to], log_recv.at[to], peer(to, place)).wait_recv()
+    lax.fori_loop(0, kv, merge_head, 0)
+    for i in order[1:]:
+        last_source(i)
 
     swap = send(square.at[0], square.at[1], square_sem.at[0], square_sem.at[1], {"tp": 1 - core})
     swap.start()

time: 89.1 us -> 82 us (0.920)
  the two profiles are of different devices: /device:TPU:25 before, /device:TPU:0 now
where the time goes in v5:
time: 82 us; the launch traced here: 81.2 us
  Pallas kernels  77 us (94%)
  local copies, waits for them, and re-layouts  3.99 us (5%)
    pallas_call x1, Pallas kernels, attend(): pl.pallas_call(functools.partial(attend_kernel, cap, plane, lines, heads...  74.9 us
    unnamed x20, local copies, waits for them, and re-layouts  3.22 us
    pallas_call x1, Pallas kernels, plan(): pl.pallas_call(functools.partial(plan_kernel, cap), out_shape=(slots, slo...  2.15 us

profile of v5, /device:TPU:0, one launch (start us, length us, event | category | flops | bytes accessed | tf_op | source)
XLA Modules:
  0.0 81.2 jit_solution(3489897223533686634)
XLA Ops:
  0.0 0.9 %copy.17 = bf16[4,2,16,4,128]{4,2,3,1,0:T(8,128)(2,1)S(1)} copy(bf16[4,2,16,4,128]{4,3,2,1,0:T(4,128)(2,1)} %param.13) | data formatting | bytes 262144 | tf_op args[2]
  0.9 0.0 copy-start.1
  0.9 0.0 copy-start.4
  1.0 0.0 copy-start.5
  1.0 0.0 copy-start.6
  1.0 0.0 copy-start.7
  1.0 2.2 %copy.16 = bf16[64,2,16,4,128]{4,2,3,1,0:T(8,128)(2,1)S(1)} copy(bf16[64,2,16,4,128]{4,3,2,1,0:T(4,128)(2,1)} %param.14) | data formatting | bytes 4194304 | tf_op args[3]
  3.2 0.0 copy-start
  3.3 0.0 copy-start.2
  3.3 0.0 copy-start.3
  3.3 0.0 copy-start.8
  3.3 0.0 copy-done.1
  3.3 0.0 copy-done.4
  3.3 0.0 copy-done.5
  3.3 0.0 copy-done.6
  3.3 0.0 copy-done.7
  3.3 2.1 %plan.1 = (s32[128]{0:T(128)S(1)}, s32[128]{0:T(128)S(1)}, bf16[4,2,4,16,128]{4,3,2,1,0:T(8,128)(2,1)S(1)}) custom-call(s32[64]{0:T(128)S(1)} %copy-done.6, s32[64]{0:T(128)S(1)} %bitcast.14, s32[4]{0:T(128)S(1)} %copy-done.4, s32[4]{0:T(128)S(1)} %copy-done.5, bf16[4,2,4,16,128]{4,3,2,1,0:T(8,128)(2,1)S(1)} %bitcast.12, ...), custom_call_target="tpu_custom_call" | custom-call | tf_op jit(solution)/shard_map/plan/pallas_call | solution.py:96
  5.5 0.0 copy-done
  5.5 0.0 copy-done.2
  5.5 0.0 copy-done.3
  5.5 0.0 copy-done.8
  5.5 74.9 %attend.1 = bf16[4,4,64,128]{3,2,1,0:T(8,128)(2,1)S(1)} custom-call(s32[128]{0:T(128)S(1)} %get-tuple-element.8.source, s32[128]{0:T(128)S(1)} %get-tuple-element.9.length, s32[4]{0:T(128)S(1)} %copy-done.8, s32[4]{0:T(128)S(1)} %copy-done.4, s32[4]{0:T(128)S(1)} %copy-done.5, bf16[4,4,64,128]{3,2,1,0:T(8,128)(2,1)S(1)} %copy-done, s32[4,128]{1,0:T(4,128)S(1)} %copy-done.3, ...), custom_call_target="tpu_custom_call" | custom-call | tf_op jit(solution)/shard_map/attend/pallas_call | solution.py:405
  80.4 0.8 reshape.11
Async XLA Ops:
  0.9 2.4 %copy-start.1 = (bf16[4,4,2,4,128]{4,3,2,1,0:T(4,128)(2,1)S(1)}, bf16[4,4,2,4,128]{4,3,2,1,0:T(4,128)(2,1)}, u32[]{:S(2)}) copy-start(bf16[4,4,2,4,128]{4,3,2,1,0:T(4,128)(2,1)} %fresh.1) | copy-start | bytes 98308
  0.9 2.4 %copy-start.4 = (s32[4]{0:T(128)S(1)}, s32[4]{0:T(128)}, u32[]{:S(2)}) copy-start(s32[4]{0:T(128)} %fill.3) | copy-start | bytes 52
  1.0 2.4 %copy-start.5 = (s32[4]{0:T(128)S(1)}, s32[4]{0:T(128)}, u32[]{:S(2)}) copy-start(s32[4]{0:T(128)} %switch.3) | copy-start | bytes 52
  1.0 2.4 %copy-start.6 = (s32[64]{0:T(128)S(1)}, s32[64]{0:T(128)}, u32[]{:S(2)}) copy-start(s32[64]{0:T(128)} %sender.1) | copy-start | bytes 772
  1.0 2.4 %copy-start.7 = (s32[64,1]{0,1:T(1,128)S(1)}, s32[64,1]{0,1:T(1,128)}, u32[]{:S(2)}) copy-start(s32[64,1]{0,1:T(1,128)} %param.19) | copy-start | bytes 772
  3.2 2.3 %copy-start = (bf16[4,4,64,128]{3,2,1,0:T(8,128)(2,1)S(1)}, bf16[4,4,64,128]{3,2,1,0:T(8,128)(2,1)}, u32[]{:S(2)}) copy-start(bf16[4,4,64,128]{3,2,1,0:T(8,128)(2,1)} %query.1) | copy-start | bytes 786436
  3.3 2.3 %copy-start.2 = (f32[8192]{0:T(1024)S(1)}, f32[8192]{0:T(1024)}, u32[]{:S(2)}) copy-start(f32[8192]{0:T(1024)} %param.21) | copy-start | bytes 98308
  3.3 2.3 %copy-start.3 = (s32[4,128]{1,0:T(4,128)S(1)}, s32[4,128]{1,0:T(4,128)}, u32[]{:S(2)}) copy-start(s32[4,128]{1,0:T(4,128)} %table.1) | copy-start | bytes 6148
  3.3 2.3 %copy-start.8 = (s32[4]{0:T(128)S(1)}, s32[4]{0:T(128)}, u32[]{:S(2)}) copy-start(s32[4]{0:T(128)} %history.1) | copy-start | bytes 52

commit v6 on v2

--- a/solution.py
+++ b/solution.py
@@ -57,33 +57,57 @@
     return scores.reshape(rows, -1)
 
 
-def pack_kernel(cap, plane, sender, target, history, fill, switch, tiles, table, out, count, bias, held):
+def pack_kernel(
+    cap, plane, sender, target, history, fill, switch, tiles, table, unfinished, fresh,
+    out, count, bias, tails, held,
+):
     replicas = out.shape[0]
     requests = fill.shape[0]
-    pool = tiles.shape[0] - requests
-    parts, kv, page, hdim = tiles.shape[1:]
+    pool, parts, kv, page, hdim = tiles.shape
     steps = bias.shape[0] // requests
     for d in range(replicas):
         held[d] = 0
     lane = lax.broadcasted_iota(jnp.int32, (page, hdim), 1)
-    out[...] = jnp.zeros_like(out)
+    offset = lax.broadcasted_iota(jnp.int32, (page, hdim), 0)
+    for g in range(requests):
+        for c in range(parts):
+            news = [fresh[s, g, c].astype(jnp.float32) for s in range(steps)]
+            for k in range(kv):
+                block = unfinished[g, c, k].astype(jnp.float32)
+                for s in range(steps):
+                    block = jnp.where(offset == fill[g] + s, news[s][k : k + 1, :], block)
+                tails[g, c, k] = block.astype(tails.dtype)
+    empty = jnp.zeros((page, hdim), out.dtype)
+    for d in range(replicas):
+        out[d, parts * kv * cap] = empty
 
     def place(e, carry):
-        d = target[e, 0]
+        d = target[e]
         rank = held[d]
         held[d] = rank + 1
         source = sender[e]
+        owner = jnp.maximum(source - pool, 0)
         for c in range(parts):
             for k in range(kv):
-                out[d, (c * kv + k) * cap + rank] = tiles[source, c, k]
-        owner = jnp.maximum(source - pool, 0)
+                out[d, (c * kv + k) * cap + rank] = jnp.where(
+                    source >= pool, tails[owner, c, k], tiles[jnp.minimum(source, pool - 1), c, k]
+                )
         length = jnp.where(source >= pool, fill[owner] + switch[owner], page)
         inside = (lane >= rank * page) & (lane < rank * page + length)
         mask = out[d, parts * kv * cap]
         out[d, parts * kv * cap] = jnp.where(inside, 1.0, mask.astype(jnp.float32)).astype(mask.dtype)
         return carry
 
+    def clear(d, carry):
+        def one(rank, carry):
+            for block in range(parts * kv):
+                out[d, block * cap + rank] = empty
+            return carry
+
+        return lax.fori_loop(held[d], cap, one, carry)
+
     lax.fori_loop(0, sender.shape[0], place, 0)
+    lax.fori_loop(0, replicas, clear, 0)
     own = counts_of(table, history, 0, pool, page)
     tail = lax.broadcasted_iota(jnp.int32, (1, requests * page), 1)
     arrivals = counts_of(table, history, pool, replicas * cap, page)
@@ -103,9 +127,9 @@
         count[line] = jnp.concatenate(rows, 0).astype(count.dtype)
 
 
-def pack(tiles, sender, target, table, history, fill, switch, steps, replicas, cap, plane):
-    pages, parts, kv, page, hdim = tiles.shape
-    requests = fill.shape[0]
+def pack(tiles, sender, target, table, history, fill, switch, unfinished, fresh, replicas, cap, plane):
+    pool, parts, kv, page, hdim = tiles.shape
+    steps, requests = fresh.shape[:2]
     smem = pl.BlockSpec(memory_space=pltpu.SMEM)
     vmem = pl.BlockSpec(memory_space=pltpu.VMEM)
     return pl.pallas_call(
@@ -113,14 +137,15 @@
         out_shape=(
             jax.ShapeDtypeStruct((replicas, parts * kv * cap + 1, page, hdim), tiles.dtype),
             jax.ShapeDtypeStruct((replicas // plane, steps * requests, plane * cap * page), jnp.bfloat16),
-            jax.ShapeDtypeStruct((steps * requests, pages * page), jnp.float32),
+            jax.ShapeDtypeStruct((steps * requests, (pool + requests) * page), jnp.float32),
+            jax.ShapeDtypeStruct(unfinished.shape, unfinished.dtype),
         ),
-        in_specs=[smem] * 5 + [vmem] * 2,
-        out_specs=(vmem, vmem, vmem),
+        in_specs=[smem] * 5 + [vmem] * 4,
+        out_specs=(vmem, vmem, vmem, vmem),
         scratch_shapes=[pltpu.SMEM((replicas,), jnp.int32)],
         compiler_params=pltpu.CompilerParams(vmem_limit_bytes=VMEM_LIMIT),
         name="pack",
-    )(sender, target, history, fill, switch, tiles, table)
+    )(sender, target, history, fill, switch, tiles, table, unfinished, fresh)
 
 
 def partial(query, keys, values, bias):
@@ -137,14 +162,14 @@
 
 def attend_kernel(
     cap, plane, lines, total_width,
-    query, count, bias, gain, tiles, outgoing,
+    query, count, bias, gain, tiles, tails, outgoing,
     out,
     arrived, asked, asked_count, answer, answer_log, given, given_log, mixed, top, total, attn, square,
     own_sem, tile_send, tile_recv, ask_send, ask_recv, count_send, count_recv,
     answer_send, answer_recv, log_send, log_recv, square_sem,
 ):
     steps, requests, heads, hdim = query.shape
-    all_pages, _, kv, page, _ = tiles.shape
+    pool, _, kv, page, _ = tiles.shape
     group = heads // kv
     groups = steps * requests
     rows = groups * group
@@ -215,9 +240,13 @@
 
     def pool_head(k, carry):
         q = query[:, :, pl.ds(k * group, group), :].reshape(rows, hdim)
-        keys = tiles[:, 0, k].reshape(all_pages * page, hdim)
-        values = tiles[:, 1, k].reshape(all_pages * page, hdim)
-        mixed[k], top[k], total[k] = partial(q, keys, values, bias[...])
+        both = [
+            jnp.concatenate(
+                [tiles[:, c, k].reshape(pool * page, hdim), tails[:, c, k].reshape(requests * page, hdim)], 0
+            )
+            for c in range(2)
+        ]
+        mixed[k], top[k], total[k] = partial(q, both[0], both[1], bias[...])
         return carry
 
     lax.fori_loop(0, kv, pool_head, 0)
@@ -341,7 +370,7 @@
                 copy.wait_send()
 
 
-def attend(query, count, bias, gain, tiles, outgoing, cap, plane):
+def attend(query, count, bias, gain, tiles, tails, outgoing, cap, plane):
     steps, requests, heads, hdim = query.shape
     kv, page = tiles.shape[2:4]
     lines = outgoing.shape[0] // plane
@@ -351,7 +380,7 @@
     return pl.pallas_call(
         functools.partial(attend_kernel, cap, plane, lines, heads * hdim * lax.axis_size("tp")),
         out_shape=jax.ShapeDtypeStruct(query.shape, jnp.bfloat16),
-        in_specs=[vmem] * 5 + [pl.BlockSpec(memory_space=pl.ANY)],
+        in_specs=[vmem] * 6 + [pl.BlockSpec(memory_space=pl.ANY)],
         out_specs=vmem,
         scratch_shapes=[
             pltpu.VMEM((lines, plane) + outgoing.shape[1:], jnp.bfloat16),
@@ -376,15 +405,7 @@
             vmem_limit_bytes=VMEM_LIMIT, collective_id=0, has_side_effects=True
         ),
         name="attend",
-    )(query, count, bias, gain, tiles, outgoing)
-
-
-def filled_tail(unfinished, fresh, fill):
-    offset = jnp.arange(unfinished.shape[2], dtype=jnp.int32)[None, None, :, None, None]
-    out = unfinished
-    for s in range(fresh.shape[0]):
-        out = jnp.where(offset == fill[:, None, None, None, None] + s, fresh[s][:, :, None], out)
-    return out
+    )(query, count, bias, gain, tiles, tails, outgoing)
 
 
 def body(query, fresh, unfinished, store, table, history, fill, sender, target, switch, gain):
@@ -392,12 +413,12 @@
     steps, requests, heads, hdim = query.shape
     cap = max(2, 2 * sender.shape[0] // replicas)
     plane = math.gcd(4, replicas)
-    tiles = jnp.concatenate([store, filled_tail(unfinished, fresh, fill)], 0)
-    tiles = jnp.transpose(tiles, (0, 1, 3, 2, 4))
-    outgoing, count, bias = pack(
-        tiles, sender, target, table, history, fill, switch, steps, replicas, cap, plane
-    )
-    normed = attend(query, count, bias, gain.reshape(heads, hdim), tiles, outgoing, cap, plane)
+    tiles = jnp.transpose(store, (0, 1, 3, 2, 4))
+    outgoing, count, bias, tails = pack(
+        tiles, sender, target.reshape(-1), table, history, fill, switch,
+        jnp.transpose(unfinished, (0, 1, 3, 2, 4)), fresh, replicas, cap, plane,
+    )
+    normed = attend(query, count, bias, gain.reshape(heads, hdim), tiles, tails, outgoing, cap, plane)
     return normed.reshape(steps, requests, heads * hdim)
 
 

time: 73.3 us -> 69.4 us (0.947)
  other arithmetic: 2.67 us -> 0 us
  local copies, waits for them, and re-layouts: 4.98 us -> 3.98 us
    select_n x1 -> x0, other arithmetic: 1.02 us -> none  [filled_tail(): jnp.where(offset == fill[:, None, None, None, None] + s, fresh[s][:, :, N...]
    eq x2 -> x0, other arithmetic: 0.8 us -> none  [filled_tail(): offset == fill[:, None, None, None, None] + s]
    broadcast_in_dim x1 -> x0, local copies, waits for them, and re-layouts: 0.76 us -> none  [filled_tail(): jnp.where(offset == fill[:, None, None, None, None] + s, fresh[s][:, :, N...]
    unnamed x16 -> x20, local copies, waits for them, and re-layouts: 3.46 us -> 3.21 us
where the time goes in v6:
time: 69.4 us; the launch traced here: 69.3 us
  Pallas kernels  65.1 us (94%)
  local copies, waits for them, and re-layouts  3.98 us (6%)
    pallas_call x1, Pallas kernels, attend(): pl.pallas_call(functools.partial(attend_kernel, cap, plane, lines, heads...  59.9 us
    pallas_call x1, Pallas kernels, pack(): pl.pallas_call(functools.partial(pack_kernel, cap, plane), out_shape=(jax...  5.21 us
    unnamed x20, local copies, waits for them, and re-layouts  3.21 us

profile of v6, /device:TPU:0, one launch (start us, length us, event | category | flops | bytes accessed | tf_op | source)
XLA Modules:
  0.0 69.3 jit_solution(15385452709522155078)
XLA Ops:
  0.0 0.9 %copy.17 = bf16[4,2,16,4,128]{4,2,3,1,0:T(8,128)(2,1)S(1)} copy(bf16[4,2,16,4,128]{4,3,2,1,0:T(4,128)(2,1)} %param.13) | data formatting | bytes 262144 | tf_op args[2]
  0.9 0.0 copy-start.1
  0.9 0.0 copy-start.3
  1.0 0.0 copy-start.4
  1.0 0.0 copy-start.5
  1.0 0.0 copy-start.6
  1.0 0.0 copy-start.7
  1.0 0.0 copy-start.8
  1.0 2.2 %copy.16 = bf16[64,2,16,4,128]{4,2,3,1,0:T(8,128)(2,1)S(1)} copy(bf16[64,2,16,4,128]{4,3,2,1,0:T(4,128)(2,1)} %param.14) | data formatting | bytes 4194304 | tf_op args[3]
  3.3 0.0 copy-start
  3.3 0.0 copy-start.2
  3.3 0.0 copy-done.1
  3.3 0.0 copy-done.3
  3.3 0.0 copy-done.4
  3.3 0.0 copy-done.5
  3.3 0.0 copy-done.6
  3.3 0.0 copy-done.7
  3.3 0.0 copy-done.8
  3.3 5.2 %pack.1 = (bf16[16,65,16,128]{3,2,1,0:T(8,128)(2,1)}, bf16[4,16,512]{2,1,0:T(8,128)(2,1)S(1)}, f32[16,1088]{1,0:T(8,128)S(1)}, bf16[4,2,4,16,128]{4,3,2,1,0:T(8,128)(2,1)S(1)}) custom-call(s32[64]{0:T(128)S(1)} %copy-done.4, s32[64]{0:T(128)S(1)} %bitcast.14, s32[4]{0:T(128)S(1)} %copy-done.6, s32[4]{0:T(128)S(1)} %copy-done.7, s32[4]{0:T(128)S(1)} %copy-done.8, ...), custom_call_target="tpu_custom_call" | custom-call | tf_op jit(solution)/shard_map/pack/pallas_call | solution.py:135
  8.6 0.0 copy-done
  8.6 0.0 copy-done.2
  8.6 59.9 %attend.1 = bf16[4,4,64,128]{3,2,1,0:T(8,128)(2,1)S(1)} custom-call(bf16[4,4,64,128]{3,2,1,0:T(8,128)(2,1)S(1)} %copy-done, bf16[4,16,512]{2,1,0:T(8,128)(2,1)S(1)} %get-tuple-element.9.count, f32[16,1088]{1,0:T(8,128)S(1)} %get-tuple-element.10.bias, f32[64,128]{1,0:T(8,128)S(1)} %bitcast.13, bf16[64,2,4,16,128]{4,3,2,1,0:T(8,128)(2,1)S(1)} %bitcast.11, ...), custom_call_target="tpu_custom_call" | custom-call | tf_op jit(solution)/shard_map/attend/pallas_call | solution.py:380
  68.5 0.8 %reshape.11 = bf16[4,4,8192]{2,1,0:T(4,128)(2,1)} reshape(bf16[4,4,64,128]{3,2,1,0:T(8,128)(2,1)S(1)} %attend.1) | data formatting | bytes 524288 | tf_op jit(solution)/shard_map/reshape | solution.py:422
Async XLA Ops:
  0.9 2.4 %copy-start.1 = (bf16[4,4,2,4,128]{4,3,2,1,0:T(4,128)(2,1)S(1)}, bf16[4,4,2,4,128]{4,3,2,1,0:T(4,128)(2,1)}, u32[]{:S(2)}) copy-start(bf16[4,4,2,4,128]{4,3,2,1,0:T(4,128)(2,1)} %fresh.1) | copy-start | bytes 98308
  0.9 2.3 %copy-start.3 = (s32[4,128]{1,0:T(4,128)S(1)}, s32[4,128]{1,0:T(4,128)}, u32[]{:S(2)}) copy-start(s32[4,128]{1,0:T(4,128)} %table.1) | copy-start | bytes 6148
  1.0 2.3 %copy-start.4 = (s32[64]{0:T(128)S(1)}, s32[64]{0:T(128)}, u32[]{:S(2)}) copy-start(s32[64]{0:T(128)} %sender.1) | copy-start | bytes 772
  1.0 2.3 %copy-start.5 = (s32[64,1]{0,1:T(1,128)S(1)}, s32[64,1]{0,1:T(1,128)}, u32[]{:S(2)}) copy-start(s32[64,1]{0,1:T(1,128)} %param.19) | copy-start | bytes 772
  1.0 2.3 %copy-start.6 = (s32[4]{0:T(128)S(1)}, s32[4]{0:T(128)}, u32[]{:S(2)}) copy-start(s32[4]{0:T(128)} %history.1) | copy-start | bytes 52
  1.0 2.3 %copy-start.7 = (s32[4]{0:T(128)S(1)}, s32[4]{0:T(128)}, u32[]{:S(2)}) copy-start(s32[4]{0:T(128)} %fill.1) | copy-start | bytes 52
  1.0 2.3 %copy-start.8 = (s32[4]{0:T(128)S(1)}, s32[4]{0:T(128)}, u32[]{:S(2)}) copy-start(s32[4]{0:T(128)} %switch.1) | copy-start | bytes 52
  3.3 5.3 %copy-start = (bf16[4,4,64,128]{3,2,1,0:T(8,128)(2,1)S(1)}, bf16[4,4,64,128]{3,2,1,0:T(8,128)(2,1)}, u32[]{:S(2)}) copy-start(bf16[4,4,64,128]{3,2,1,0:T(8,128)(2,1)} %query.1) | copy-start | bytes 786436
  3.3 5.3 %copy-start.2 = (f32[8192]{0:T(1024)S(1)}, f32[8192]{0:T(1024)}, u32[]{:S(2)}) copy-start(f32[8192]{0:T(1024)} %param.21) | copy-start | bytes 98308

commit v7 on v6

--- a/solution.py
+++ b/solution.py
@@ -58,13 +58,12 @@
 
 
 def pack_kernel(
-    cap, plane, sender, target, history, fill, switch, tiles, table, unfinished, fresh,
-    out, count, bias, tails, held,
+    cap, sender, target, fill, switch, tiles, unfinished, fresh, out, tails, held,
 ):
     replicas = out.shape[0]
     requests = fill.shape[0]
     pool, parts, kv, page, hdim = tiles.shape
-    steps = bias.shape[0] // requests
+    steps = fresh.shape[0]
     for d in range(replicas):
         held[d] = 0
     lane = lax.broadcasted_iota(jnp.int32, (page, hdim), 1)
@@ -108,44 +107,24 @@
 
     lax.fori_loop(0, sender.shape[0], place, 0)
     lax.fori_loop(0, replicas, clear, 0)
-    own = counts_of(table, history, 0, pool, page)
-    tail = lax.broadcasted_iota(jnp.int32, (1, requests * page), 1)
-    arrivals = counts_of(table, history, pool, replicas * cap, page)
-    width = plane * cap * page
-    for t in range(steps):
-        for g in range(requests):
-            row = t * requests + g
-            bias[row : row + 1, : pool * page] = bias_of(own[g])
-            seen = (tail // page == g) & (tail % page < fill[g] + t + 1)
-            bias[row : row + 1, pool * page :] = jnp.where(seen, 0.0, NEG)
-    for line in range(replicas // plane):
-        rows = []
-        for t in range(steps):
-            for g in range(requests):
-                part = arrivals[g][:, line * width : (line + 1) * width]
-                rows.append(jnp.where(t >= switch[g], part, 0.0))
-        count[line] = jnp.concatenate(rows, 0).astype(count.dtype)
-
-
-def pack(tiles, sender, target, table, history, fill, switch, unfinished, fresh, replicas, cap, plane):
+
+
+def pack(tiles, sender, target, fill, switch, unfinished, fresh, replicas, cap):
     pool, parts, kv, page, hdim = tiles.shape
-    steps, requests = fresh.shape[:2]
     smem = pl.BlockSpec(memory_space=pltpu.SMEM)
     vmem = pl.BlockSpec(memory_space=pltpu.VMEM)
     return pl.pallas_call(
-        functools.partial(pack_kernel, cap, plane),
+        functools.partial(pack_kernel, cap),
         out_shape=(
             jax.ShapeDtypeStruct((replicas, parts * kv * cap + 1, page, hdim), tiles.dtype),
-            jax.ShapeDtypeStruct((replicas // plane, steps * requests, plane * cap * page), jnp.bfloat16),
-            jax.ShapeDtypeStruct((steps * requests, (pool + requests) * page), jnp.float32),
             jax.ShapeDtypeStruct(unfinished.shape, unfinished.dtype),
         ),
-        in_specs=[smem] * 5 + [vmem] * 4,
-        out_specs=(vmem, vmem, vmem, vmem),
+        in_specs=[smem] * 4 + [vmem] * 3,
+        out_specs=(vmem, vmem),
         scratch_shapes=[pltpu.SMEM((replicas,), jnp.int32)],
         compiler_params=pltpu.CompilerParams(vmem_limit_bytes=VMEM_LIMIT),
         name="pack",
-    )(sender, target, history, fill, switch, tiles, table, unfinished, fresh)
+    )(sender, target, fill, switch, tiles, unfinished, fresh)
 
 
 def partial(query, keys, values, bias):
@@ -162,9 +141,10 @@
 
 def attend_kernel(
     cap, plane, lines, total_width,
-    query, count, bias, gain, tiles, tails, outgoing,
+    history, fill, switch,
+    query, table, gain, tiles, tails, outgoing,
     out,
-    arrived, asked, asked_count, answer, answer_log, given, given_log, mixed, top, total, attn, square,
+    count, bias, arrived, asked, asked_count, answer, answer_log, given, given_log, mixed, top, total, attn, square,
     own_sem, tile_send, tile_recv, ask_send, ask_recv, count_send, count_recv,
     answer_send, answer_recv, log_send, log_recv, square_sem,
 ):
@@ -206,9 +186,12 @@
 
     def ask(j):
         to = line_at(j)
-        return (
-            send(query, asked.at[line], ask_send.at[to], ask_recv.at[line], peer(to, place)),
-            send(count.at[to], asked_count.at[line], count_send.at[to], count_recv.at[line], peer(to, place)),
+        return send(query, asked.at[line], ask_send.at[to], ask_recv.at[line], peer(to, place))
+
+    def ask_counts(j):
+        to = line_at(j)
+        return send(
+            count.at[to], asked_count.at[line], count_send.at[to], count_recv.at[line], peer(to, place)
         )
 
     def ship(j, i):
@@ -230,13 +213,40 @@
             send(answer_log.at[to], given_log.at[line], log_send.at[to], log_recv.at[line], peer(to, place)),
         )
 
-    for j in range(1, lines + 1):
+    def launch(j):
         for i in range(1, plane):
             ship(j, i).start()
         keep(j).start()
-        if j < lines:
-            for copy in ask(lines - j):
-                copy.start()
+
+    if lines > 1:
+        launch(1)
+    for j in range(1, lines):
+        ask(lines - j).start()
+
+    tokens_in = counts_of(table, history, pool, lines * plane * cap, page)
+    for to in range(lines):
+        parts_of = [
+            jnp.where(t >= switch[g], tokens_in[g][:, to * tokens : (to + 1) * tokens], 0.0)
+            for t in range(steps)
+            for g in range(requests)
+        ]
+        count[to] = jnp.concatenate(parts_of, 0).astype(count.dtype)
+    for j in range(1, lines):
+        ask_counts(lines - j).start()
+    for j in range(2, lines):
+        launch(j)
+    keep(lines).start()
+    for i in range(lines, plane):
+        ship(lines, i).start()
+
+    own = counts_of(table, history, 0, pool, page)
+    tail = lax.broadcasted_iota(jnp.int32, (1, requests * page), 1)
+    for t in range(steps):
+        for g in range(requests):
+            row = t * requests + g
+            bias[row : row + 1, : pool * page] = bias_of(own[g])
+            seen = (tail // page == g) & (tail % page < fill[g] + t + 1)
+            bias[row : row + 1, pool * page :] = jnp.where(seen, 0.0, NEG)
 
     def pool_head(k, carry):
         q = query[:, :, pl.ds(k * group, group), :].reshape(rows, hdim)
@@ -300,35 +310,13 @@
         lax.fori_loop(0, kv, set_head, 0)
         for copy in reply(j):
             copy.start()
-
-    for i in range(1, plane):
-        source = place_at(i)
-        send(
-            outgoing.at[0], arrived.at[line, source], tile_send.at[line, source], tile_recv.at[line, source],
-            peer(line, source),
-        ).wait_recv()
-    keep(lines).wait()
-    last_bias = bias_of(count[line].astype(jnp.float32) * filled(line))
-
-    def last_head(k, carry):
-        q = query[:, :, pl.ds(k * group, group), :].reshape(rows, hdim)
-        keys, values = arrivals(line, k)
-        part, best, amount = partial(q, keys, values, last_bias)
-        high = jnp.maximum(best, top[k])
-        fresh, old = jnp.exp2(best - high), jnp.exp2(top[k] - high)
-        mixed[k] = part * fresh + mixed[k] * old
-        total[k] = amount * fresh + total[k] * old
-        top[k] = high
-        return carry
-
-    lax.fori_loop(0, kv, last_head, 0)
+        if j < plane:
+            ship(lines, j).start()
 
     for j in range(1, lines):
         to = line_at(j)
         send(answer.at[to], given.at[to], answer_send.at[to], answer_recv.at[to], peer(to, place)).wait_recv()
         send(answer_log.at[to], given_log.at[to], log_send.at[to], log_recv.at[to], peer(to, place)).wait_recv()
-
-    square[0] = jnp.zeros_like(square[0])
 
     def merge_head(k, carry):
         logs = []
@@ -344,13 +332,35 @@
             share = jnp.exp2(logs[j - 1] - high)
             whole = whole + given[line_at(j), k].astype(jnp.float32) * share
             amount = amount + share
-        result = (whole / amount).astype(jnp.bfloat16)
+        mixed[k], total[k], top[k] = whole, amount, high
+        return carry
+
+    lax.fori_loop(0, kv, merge_head, 0)
+    square[0] = jnp.zeros_like(square[0])
+
+    for i in range(1, plane):
+        source = place_at(i)
+        send(
+            outgoing.at[0], arrived.at[line, source], tile_send.at[line, source], tile_recv.at[line, source],
+            peer(line, source),
+        ).wait_recv()
+    keep(lines).wait()
+    last_bias = bias_of(count[line].astype(jnp.float32) * filled(line))
+
+    def last_head(k, carry):
+        q = query[:, :, pl.ds(k * group, group), :].reshape(rows, hdim)
+        keys, values = arrivals(line, k)
+        part, best, amount = partial(q, keys, values, last_bias)
+        high = jnp.maximum(best, top[k])
+        fresh, old = jnp.exp2(best - high), jnp.exp2(top[k] - high)
+        whole = part * fresh + mixed[k] * old
+        result = (whole / (amount * fresh + total[k] * old)).astype(jnp.bfloat16)
         attn[:, :, pl.ds(k * group, group), :] = result.reshape(steps, requests, group, hdim)
         wide = result.astype(jnp.float32)
         square[0] += jnp.sum((wide * wide).reshape(groups, group, hdim), axis=1)
         return carry
 
-    lax.fori_loop(0, kv, merge_head, 0)
+    lax.fori_loop(0, kv, last_head, 0)
     swap = send(square.at[0], square.at[1], square_sem.at[0], square_sem.at[1], {"tp": 1 - core})
     swap.start()
     swap.wait()
@@ -366,26 +376,30 @@
         for i in range(1, plane):
             ship(j, i).wait_send()
         if j < lines:
-            for copy in ask(j) + reply(j):
+            for copy in (ask(j), ask_counts(j)) + reply(j):
                 copy.wait_send()
 
 
-def attend(query, count, bias, gain, tiles, tails, outgoing, cap, plane):
+def attend(history, fill, switch, query, table, gain, tiles, tails, outgoing, cap, plane):
     steps, requests, heads, hdim = query.shape
     kv, page = tiles.shape[2:4]
     lines = outgoing.shape[0] // plane
     rows = steps * requests * heads // kv
+    counts = (lines, steps * requests, plane * cap * page)
+    smem = pl.BlockSpec(memory_space=pltpu.SMEM)
     vmem = pl.BlockSpec(memory_space=pltpu.VMEM)
     dma = pltpu.SemaphoreType.DMA
     return pl.pallas_call(
         functools.partial(attend_kernel, cap, plane, lines, heads * hdim * lax.axis_size("tp")),
         out_shape=jax.ShapeDtypeStruct(query.shape, jnp.bfloat16),
-        in_specs=[vmem] * 6 + [pl.BlockSpec(memory_space=pl.ANY)],
+        in_specs=[smem] * 3 + [vmem] * 5 + [pl.BlockSpec(memory_space=pl.ANY)],
         out_specs=vmem,
         scratch_shapes=[
+            pltpu.VMEM(counts, jnp.bfloat16),
+            pltpu.VMEM((steps * requests, (tiles.shape[0] + requests) * page), jnp.float32),
             pltpu.VMEM((lines, plane) + outgoing.shape[1:], jnp.bfloat16),
             pltpu.VMEM((lines,) + query.shape, jnp.bfloat16),
-            pltpu.VMEM(count.shape, jnp.bfloat16),
+            pltpu.VMEM(counts, jnp.bfloat16),
             pltpu.VMEM((lines, kv, rows, hdim), jnp.bfloat16),
             pltpu.VMEM((lines, kv, 1, rows), jnp.float32),
             pltpu.VMEM((lines, kv, rows, hdim), jnp.bfloat16),
@@ -405,7 +419,7 @@
             vmem_limit_bytes=VMEM_LIMIT, collective_id=0, has_side_effects=True
         ),
         name="attend",
-    )(query, count, bias, gain, tiles, tails, outgoing)
+    )(history, fill, switch, query, table, gain, tiles, tails, outgoing)
 
 
 def body(query, fresh, unfinished, store, table, history, fill, sender, target, switch, gain):
@@ -414,11 +428,13 @@
     cap = max(2, 2 * sender.shape[0] // replicas)
     plane = math.gcd(4, replicas)
     tiles = jnp.transpose(store, (0, 1, 3, 2, 4))
-    outgoing, count, bias, tails = pack(
-        tiles, sender, target.reshape(-1), table, history, fill, switch,
-        jnp.transpose(unfinished, (0, 1, 3, 2, 4)), fresh, replicas, cap, plane,
-    )
-    normed = attend(query, count, bias, gain.reshape(heads, hdim), tiles, tails, outgoing, cap, plane)
+    outgoing, tails = pack(
+        tiles, sender, target.reshape(-1), fill, switch,
+        jnp.transpose(unfinished, (0, 1, 3, 2, 4)), fresh, replicas, cap,
+    )
+    normed = attend(
+        history, fill, switch, query, table, gain.reshape(heads, hdim), tiles, tails, outgoing, cap, plane
+    )
     return normed.reshape(steps, requests, heads * hdim)
 
 

time: 69.4 us -> 81.6 us (1.18)
  the two profiles are of different devices: /device:TPU:0 before, /device:TPU:25 now
where the time goes in v7:
time: 81.6 us; the launch traced here: 81.4 us
  Pallas kernels  77.3 us (95%)
  local copies, waits for them, and re-layouts  3.96 us (5%)
    pallas_call x1, Pallas kernels, attend(): pl.pallas_call(functools.partial(attend_kernel, cap, plane, lines, heads...  72.6 us
    pallas_call x1, Pallas kernels, pack(): pl.pallas_call(functools.partial(pack_kernel, cap), out_shape=(jax.ShapeD...  4.64 us
    unnamed x20, local copies, waits for them, and re-layouts  3.19 us

profile of v7, /device:TPU:25, one launch (start us, length us, event | category | flops | bytes accessed | tf_op | source)
XLA Modules:
  0.0 81.4 jit_solution(4069935246644173878)
XLA Ops:
  0.0 0.9 %copy.17 = bf16[4,2,16,4,128]{4,2,3,1,0:T(8,128)(2,1)S(1)} copy(bf16[4,2,16,4,128]{4,3,2,1,0:T(4,128)(2,1)} %param.13) | data formatting | bytes 262144 | tf_op args[2]
  0.9 0.0 copy-start.1
  0.9 0.0 copy-start.4
  1.0 0.0 copy-start.5
  1.0 0.0 copy-start.6
  1.0 0.0 copy-start.7
  1.0 2.2 %copy.16 = bf16[64,2,16,4,128]{4,2,3,1,0:T(8,128)(2,1)S(1)} copy(bf16[64,2,16,4,128]{4,3,2,1,0:T(4,128)(2,1)} %param.14) | data formatting | bytes 4194304 | tf_op args[3]
  3.2 0.0 copy-start
  3.2 0.0 copy-start.2
  3.2 0.0 copy-start.3
  3.2 0.0 copy-start.8
  3.3 0.0 copy-done.1
  3.3 0.0 copy-done.4
  3.3 0.0 copy-done.5
  3.3 0.0 copy-done.6
  3.3 0.0 copy-done.7
  3.3 4.6 %pack.1 = (bf16[16,65,16,128]{3,2,1,0:T(8,128)(2,1)}, bf16[4,2,4,16,128]{4,3,2,1,0:T(8,128)(2,1)S(1)}) custom-call(s32[64]{0:T(128)S(1)} %copy-done.6, s32[64]{0:T(128)S(1)} %bitcast.14, s32[4]{0:T(128)S(1)} %copy-done.4, s32[4]{0:T(128)S(1)} %copy-done.5, bf16[64,2,4,16,128]{4,3,2,1,0:T(8,128)(2,1)S(1)} %bitcast.10, ...), custom_call_target="tpu_custom_call" | custom-call | tf_op jit(solution)/shard_map/pack/pallas_call | solution.py:116
  8.0 0.0 copy-done
  8.0 0.0 copy-done.2
  8.0 0.0 copy-done.3
  8.0 0.0 copy-done.8
  8.0 72.6 %attend.1 = bf16[4,4,64,128]{3,2,1,0:T(8,128)(2,1)S(1)} custom-call(s32[4]{0:T(128)S(1)} %copy-done.8, s32[4]{0:T(128)S(1)} %copy-done.4, s32[4]{0:T(128)S(1)} %copy-done.5, bf16[4,4,64,128]{3,2,1,0:T(8,128)(2,1)S(1)} %copy-done, s32[4,128]{1,0:T(4,128)S(1)} %copy-done.3, f32[64,128]{1,0:T(8,128)S(1)} %bitcast.13, bf16[64,2,4,16,128]{4,3,2,1,0:T(8,128)(2,1)S(1)} %bitcast.11, ...), custom_call_target="tpu_custom_call" | custom-call | tf_op jit(solution)/shard_map/attend/pallas_call | solution.py:392
  80.6 0.8 reshape.11
Async XLA Ops:
  0.9 2.3 %copy-start.1 = (bf16[4,4,2,4,128]{4,3,2,1,0:T(4,128)(2,1)S(1)}, bf16[4,4,2,4,128]{4,3,2,1,0:T(4,128)(2,1)}, u32[]{:S(2)}) copy-start(bf16[4,4,2,4,128]{4,3,2,1,0:T(4,128)(2,1)} %fresh.1) | copy-start | bytes 98308
  0.9 2.3 %copy-start.4 = (s32[4]{0:T(128)S(1)}, s32[4]{0:T(128)}, u32[]{:S(2)}) copy-start(s32[4]{0:T(128)} %fill.3) | copy-start | bytes 52
  1.0 2.3 %copy-start.5 = (s32[4]{0:T(128)S(1)}, s32[4]{0:T(128)}, u32[]{:S(2)}) copy-start(s32[4]{0:T(128)} %switch.3) | copy-start | bytes 52
  1.0 2.3 %copy-start.6 = (s32[64]{0:T(128)S(1)}, s32[64]{0:T(128)}, u32[]{:S(2)}) copy-start(s32[64]{0:T(128)} %sender.1) | copy-start | bytes 772
  1.0 2.3 %copy-start.7 = (s32[64,1]{0,1:T(1,128)S(1)}, s32[64,1]{0,1:T(1,128)}, u32[]{:S(2)}) copy-start(s32[64,1]{0,1:T(1,128)} %param.19) | copy-start | bytes 772
  3.2 4.7 %copy-start = (bf16[4,4,64,128]{3,2,1,0:T(8,128)(2,1)S(1)}, bf16[4,4,64,128]{3,2,1,0:T(8,128)(2,1)}, u32[]{:S(2)}) copy-start(bf16[4,4,64,128]{3,2,1,0:T(8,128)(2,1)} %query.1) | copy-start | bytes 786436
  3.2 4.7 %copy-start.2 = (f32[8192]{0:T(1024)S(1)}, f32[8192]{0:T(1024)}, u32[]{:S(2)}) copy-start(f32[8192]{0:T(1024)} %param.21) | copy-start | bytes 98308
  3.2 4.7 %copy-start.3 = (s32[4,128]{1,0:T(4,128)S(1)}, s32[4,128]{1,0:T(4,128)}, u32[]{:S(2)}) copy-start(s32[4,128]{1,0:T(4,128)} %table.1) | copy-start | bytes 6148
  3.2 4.7 %copy-start.8 = (s32[4]{0:T(128)S(1)}, s32[4]{0:T(128)}, u32[]{:S(2)}) copy-start(s32[4]{0:T(128)} %history.1) | copy-start | bytes 52

commit v8 on v6

--- a/solution.py
+++ b/solution.py
@@ -194,6 +194,11 @@
         return lax.rem(line + lines - step, lines)
 
     def place_at(step):
+        if plane == 4:
+            if step in (1, 2):
+                step = step + core * (3 - 2 * step)
+            y, x = lax.div(place, 2), lax.rem(place, 2)
+            return lax.rem(y + step // 2, 2) * 2 + lax.rem(x + step % 2, 2)
         return lax.rem(place + step, plane)
 
     barrier = pltpu.get_barrier_semaphore()

time: 69.4 us -> 70.3 us (1.013)
  Pallas kernels: 65.1 us -> 66.1 us
    pallas_call x1, Pallas kernels: 59.9 us -> 60.9 us  [attend(): pl.pallas_call(functools.partial(attend_kernel, cap, plane, lines, heads...]
where the time goes in v8:
time: 70.3 us; the launch traced here: 70.2 us
  Pallas kernels  66.1 us (94%)
  local copies, waits for them, and re-layouts  3.98 us (6%)
    pallas_call x1, Pallas kernels, attend(): pl.pallas_call(functools.partial(attend_kernel, cap, plane, lines, heads...  60.9 us
    pallas_call x1, Pallas kernels, pack(): pl.pallas_call(functools.partial(pack_kernel, cap, plane), out_shape=(jax...  5.21 us
    unnamed x20, local copies, waits for them, and re-layouts  3.21 us

profile of v8, /device:TPU:0, one launch (start us, length us, event | category | flops | bytes accessed | tf_op | source)
XLA Modules:
  0.0 70.2 jit_solution(3520652053921931480)
XLA Ops:
  0.0 0.9 %copy.17 = bf16[4,2,16,4,128]{4,2,3,1,0:T(8,128)(2,1)S(1)} copy(bf16[4,2,16,4,128]{4,3,2,1,0:T(4,128)(2,1)} %param.13) | data formatting | bytes 262144 | tf_op args[2]
  0.9 0.0 copy-start.1
  0.9 0.0 copy-start.3
  1.0 0.0 copy-start.4
  1.0 0.0 copy-start.5
  1.0 0.0 copy-start.6
  1.0 0.0 copy-start.7
  1.0 0.0 copy-start.8
  1.0 2.2 %copy.16 = bf16[64,2,16,4,128]{4,2,3,1,0:T(8,128)(2,1)S(1)} copy(bf16[64,2,16,4,128]{4,3,2,1,0:T(4,128)(2,1)} %param.14) | data formatting | bytes 4194304 | tf_op args[3]
  3.3 0.0 copy-start
  3.3 0.0 copy-start.2
  3.3 0.0 copy-done.1
  3.3 0.0 copy-done.3
  3.3 0.0 copy-done.4
  3.3 0.0 copy-done.5
  3.3 0.0 copy-done.6
  3.3 0.0 copy-done.7
  3.3 0.0 copy-done.8
  3.3 5.2 %pack.1 = (bf16[16,65,16,128]{3,2,1,0:T(8,128)(2,1)}, bf16[4,16,512]{2,1,0:T(8,128)(2,1)S(1)}, f32[16,1088]{1,0:T(8,128)S(1)}, bf16[4,2,4,16,128]{4,3,2,1,0:T(8,128)(2,1)S(1)}) custom-call(s32[64]{0:T(128)S(1)} %copy-done.4, s32[64]{0:T(128)S(1)} %bitcast.14, s32[4]{0:T(128)S(1)} %copy-done.6, s32[4]{0:T(128)S(1)} %copy-done.7, s32[4]{0:T(128)S(1)} %copy-done.8, ...), custom_call_target="tpu_custom_call" | custom-call | tf_op jit(solution)/shard_map/pack/pallas_call | solution.py:135
  8.6 0.0 copy-done
  8.6 0.0 copy-done.2
  8.6 60.9 %attend.1 = bf16[4,4,64,128]{3,2,1,0:T(8,128)(2,1)S(1)} custom-call(bf16[4,4,64,128]{3,2,1,0:T(8,128)(2,1)S(1)} %copy-done, bf16[4,16,512]{2,1,0:T(8,128)(2,1)S(1)} %get-tuple-element.9.count, f32[16,1088]{1,0:T(8,128)S(1)} %get-tuple-element.10.bias, f32[64,128]{1,0:T(8,128)S(1)} %bitcast.13, bf16[64,2,4,16,128]{4,3,2,1,0:T(8,128)(2,1)S(1)} %bitcast.11, ...), custom_call_target="tpu_custom_call" | custom-call | tf_op jit(solution)/shard_map/attend/pallas_call | solution.py:385
  69.4 0.8 %reshape.11 = bf16[4,4,8192]{2,1,0:T(4,128)(2,1)} reshape(bf16[4,4,64,128]{3,2,1,0:T(8,128)(2,1)S(1)} %attend.1) | data formatting | bytes 524288 | tf_op jit(solution)/shard_map/reshape | solution.py:427
Async XLA Ops:
  0.9 2.4 %copy-start.1 = (bf16[4,4,2,4,128]{4,3,2,1,0:T(4,128)(2,1)S(1)}, bf16[4,4,2,4,128]{4,3,2,1,0:T(4,128)(2,1)}, u32[]{:S(2)}) copy-start(bf16[4,4,2,4,128]{4,3,2,1,0:T(4,128)(2,1)} %fresh.1) | copy-start | bytes 98308
  0.9 2.3 %copy-start.3 = (s32[4,128]{1,0:T(4,128)S(1)}, s32[4,128]{1,0:T(4,128)}, u32[]{:S(2)}) copy-start(s32[4,128]{1,0:T(4,128)} %table.1) | copy-start | bytes 6148
  1.0 2.3 %copy-start.4 = (s32[64]{0:T(128)S(1)}, s32[64]{0:T(128)}, u32[]{:S(2)}) copy-start(s32[64]{0:T(128)} %sender.1) | copy-start | bytes 772
  1.0 2.3 %copy-start.5 = (s32[64,1]{0,1:T(1,128)S(1)}, s32[64,1]{0,1:T(1,128)}, u32[]{:S(2)}) copy-start(s32[64,1]{0,1:T(1,128)} %param.19) | copy-start | bytes 772
  1.0 2.3 %copy-start.6 = (s32[4]{0:T(128)S(1)}, s32[4]{0:T(128)}, u32[]{:S(2)}) copy-start(s32[4]{0:T(128)} %history.1) | copy-start | bytes 52
  1.0 2.3 %copy-start.7 = (s32[4]{0:T(128)S(1)}, s32[4]{0:T(128)}, u32[]{:S(2)}) copy-start(s32[4]{0:T(128)} %fill.1) | copy-start | bytes 52
  1.0 2.3 %copy-start.8 = (s32[4]{0:T(128)S(1)}, s32[4]{0:T(128)}, u32[]{:S(2)}) copy-start(s32[4]{0:T(128)} %switch.1) | copy-start | bytes 52
  3.3 5.3 %copy-start = (bf16[4,4,64,128]{3,2,1,0:T(8,128)(2,1)S(1)}, bf16[4,4,64,128]{3,2,1,0:T(8,128)(2,1)}, u32[]{:S(2)}) copy-start(bf16[4,4,64,128]{3,2,1,0:T(8,128)(2,1)} %query.1) | copy-start | bytes 786436
  3.3 5.3 %copy-start.2 = (f32[8192]{0:T(1024)S(1)}, f32[8192]{0:T(1024)}, u32[]{:S(2)}) copy-start(f32[8192]{0:T(1024)} %param.21) | copy-start | bytes 98308
